TPU v7x, 32 devices: a whole 2x2x4 slice. The times are simulated.
32 devices in a mesh: seq: 8 (over z, core), chan: 4 (over y, x).
Axes of the slice: x: 2, y: 2, z: 4, core: 2. Of those that a mesh axis runs over, the one named last changes fastest.
Arguments:
- tokens: bfloat16 [16384, 768], P(('seq', 'chan')), may hold values from -6 to 6
- norm_gain: float32 [768], replicated, may hold values from 0.5 to 1.5
- in_weight: bfloat16 [768, 3072], replicated, may hold values from -0.21875 to 0.21875
- conv_weight: float32 [4, 1536], P(None, 'chan'), may hold values from -3 to 3
- conv_bias: float32 [1536], P('chan'), may hold values from -3 to 3
- proj_weight: bfloat16 [1536, 80], P('chan'), may hold values from -0.15625 to 0.15625
- step_weight: bfloat16 [48, 1536], P(None, 'chan'), may hold values from -0.875 to 0.875
- step_bias: float32 [1536], P('chan'), may hold values from -6 to -1
- decay_log: float32 [16, 1536], P(None, 'chan'), may hold values from -3 to 2.5
- skip_gain: float32 [1536], P('chan'), may hold values from 0.5 to 1.5
- out_weight: bfloat16 [1536, 768], replicated, may hold values from -0.078125 to 0.078125
- cotangent: bfloat16 [16384, 768], P(('seq', 'chan')), may hold values from -6 to 6
- lengths: int32 [8, 4], P('seq'), may hold values from 64 to 1856, as said below
Outputs:
- block_out: bfloat16 [16384, 768], P(('seq', 'chan'))
- grad_tokens: float32 [16384, 768], P(('seq', 'chan'))
- grad_norm_gain: float32 [768], P('chan')
- grad_in_weight: float32 [768, 3072], P(None, 'chan')
- grad_conv_weight: float32 [4, 1536], P(None, 'chan')
- grad_conv_bias: float32 [1536], P('chan')
- grad_proj_weight: float32 [1536, 80], P('chan')
- grad_step_weight: float32 [48, 1536], P(None, 'chan')
- grad_step_bias: float32 [1536], P('chan')
- grad_decay_log: float32 [16, 1536], P(None, 'chan')
- grad_skip_gain: float32 [1536], P('chan')
- grad_out_weight: float32 [1536, 768], P('chan')
Inputs may be any that keep to these rules, and one draw needn't show every extreme that they name: Each row lists the lengths of the 4 sequences of one group in packing order; they sum to 2048. One, the long one, begins within the group's first 512 rows and ends within its last 512 rows; the others are at most 128 long.
All inputs are finite; a program needn't handle non-finite values.
Results may differ from a plain program's by a relative error of at most 0.011.
Values may be sent and summed in bfloat16 or wider, within the bound.
A program may use at most 320 MiB of HBM per device.

v0:
```python
import functools
import math

import jax
import jax.numpy as jnp
from jax import lax
from jax.experimental import pallas as pl
from jax.experimental.pallas import tpu as pltpu
from jax.sharding import PartitionSpec as P

epsilon = 1e-05
LOG2E = math.log2(math.e)
CUT = 1e30
TC = 16
EB = 384
RT = 32
BLOCK_SLOTS = 4
HALO = 16
PAR = 24
WTS = 128
f32 = jnp.float32
bf16 = jnp.bfloat16
NT = (((1,), (1,)), ((), ()))
TN = (((0,), (0,)), ((), ()))


def params(**more):
    return pltpu.CompilerParams(vmem_limit_bytes=60 * 1024 * 1024, **more)


def cols(rows, width=EB, shift=0):
    return pl.BlockSpec((rows, width), lambda i: (0, i + shift))


def tall(rows, width, shift=0):
    return pl.BlockSpec((rows, width), lambda i: (i + shift, 0))


def lead(rows, width, count=1):
    return pl.BlockSpec((count, rows, width), lambda i: (i, 0, 0))


def whole(*shape):
    return pl.BlockSpec(shape, lambda i: (0,) * len(shape))


def once(*shape):
    return pl.BlockSpec(shape, lambda i: (0,) * len(shape), pipeline_mode=pl.Buffered(1))


def shape(dtype, *dims):
    return jax.ShapeDtypeStruct(dims, dtype)


def row_tiles(count, body):
    def step(i, unused):
        body(pl.multiple_of(i * RT, RT))
        return unused

    lax.fori_loop(0, count // RT, step, 0)


def same_step(states, rows):
    dims = (rows, TC * states)
    here = lax.rem(lax.broadcasted_iota(jnp.int32, dims, 0), TC) * states
    place = lax.broadcasted_iota(jnp.int32, dims, 1)
    return (place >= here) & (place < here + states)


class Layout:
    def __init__(self, R, N, K):
        self.R, self.N, self.K = R, N, K
        self.step = R + 2 * N
        self.decay = 0
        self.conv = self.decay + N
        self.conv_b = self.conv + K
        self.step_b = self.conv_b + 1
        self.skip = self.step_b + 1
        self.end = self.skip + 1


def start_gather(
    L, count, cw_ref, cb_ref, pw_ref, sw_ref, sb_ref, dl_ref, sk_ref, tok_ref,
    wts_ref, par_ref, halo_ref, send_sem, recv_sem, halo_sems,
):
    si, ci = lax.axis_index("seq"), lax.axis_index("chan")
    T = tok_ref.shape[0]
    width = par_ref.shape[2]
    barrier = pltpu.get_barrier_semaphore()
    for k in range(1, count):
        pl.semaphore_signal(
            barrier, inc=1, device_id=(si, lax.rem(ci + k, count)),
            device_id_type=pl.DeviceIdType.MESH,
        )
    own, weights = par_ref.at[ci], wts_ref.at[ci]
    weights[...] = jnp.concatenate(
        [pw_ref[...].astype(f32), sw_ref[...].astype(f32)], axis=0
    ).astype(bf16)
    own[...] = jnp.concatenate(
        [
            dl_ref[...], cw_ref[...], cb_ref[...].reshape(1, width), sb_ref[...].reshape(1, width),
            sk_ref[...].reshape(1, width), jnp.zeros((PAR - L.end, width), f32),
        ],
        axis=0,
    )
    pl.semaphore_wait(barrier, count - 1)

    def share(ref, j, k):
        return pltpu.make_async_remote_copy(
            src_ref=ref, dst_ref=ref, send_sem=send_sem.at[j, k], recv_sem=recv_sem.at[j, k],
            device_id=(si, lax.rem(ci + k, count)), device_id_type=pl.DeviceIdType.MESH,
        )

    edge = pltpu.make_async_remote_copy(
        src_ref=tok_ref.at[pl.ds(T - HALO, HALO)], dst_ref=halo_ref,
        send_sem=halo_sems.at[0], recv_sem=halo_sems.at[1],
        device_id=(si, lax.rem(ci + 1, count)), device_id_type=pl.DeviceIdType.MESH,
    )
    edge.start()
    for j, ref in enumerate((own, weights)):
        for k in range(1, count):
            share(ref, j, k).start()

    def wait():
        edge.wait()
        for j, ref in enumerate((own, weights)):
            for k in range(1, count):
                share(ref, j, k).wait()

    return wait


def gather_kernel(L, count, *refs):
    start_gather(L, count, *refs)()


def gather_scratch(count):
    return [
        pltpu.SemaphoreType.DMA((2, count)),
        pltpu.SemaphoreType.DMA((2, count)),
        pltpu.SemaphoreType.DMA((2,)),
    ]


def gather_params(L, count, parts, tokens):
    width = parts[0].shape[1]
    T, D = tokens.shape
    vmem = pl.BlockSpec(memory_space=pltpu.VMEM)
    return pl.pallas_call(
        functools.partial(gather_kernel, L, count),
        in_specs=[vmem] * 8,
        out_specs=[vmem] * 3,
        out_shape=[shape(bf16, count, WTS, width), shape(f32, count, PAR, width), shape(bf16, HALO, D)],
        scratch_shapes=gather_scratch(count),
        compiler_params=params(collective_id=1, has_side_effects=True),
        name="gather_params",
    )(*parts, tokens)


def front_kernel(
    L, count, inside, len_ref, tok_ref, gain_ref, wi_ref, wg_ref, wo_ref, cot_ref, *refs,
):
    given, refs = refs[: 7 if inside else 3], refs[7 if inside else 3 :]
    (
        marks_ref, normed_ref, inner_ref, gate_ref, gg_ref, g_ref, cs_ref, act_ref, proj_ref, bch_ref, cch_ref,
    ) = refs[:11]
    results, refs = refs[11 : 13 if inside else 11], refs[13 if inside else 11 :]
    hn_ref, xs_ref, low_ref = refs[:3]
    T = tok_ref.shape[0]
    N, K = L.N, L.K
    i = pl.program_id(0)
    sub = low_ref.shape[1] // EB
    if inside:
        wts_ref, par_ref, halo_ref, *sems = refs[3:]
        first = i * sub
    else:
        wts_ref, par_ref, halo_ref = given
        first = 0

    def norm(x):
        x = x.astype(f32)
        inv = lax.rsqrt(jnp.mean(x * x, axis=1, keepdims=True) + epsilon)
        return (x * inv * gain_ref[...].reshape(1, x.shape[1])).astype(bf16)

    def products():
        low = jnp.dot(normed_ref[...], wi_ref[...], preferred_element_type=f32).astype(bf16)
        inner_ref[HALO:, :] = low
        xs_ref[HALO:, :] = low.astype(f32)
        gate_ref[...] = jnp.dot(normed_ref[...], wg_ref[...], preferred_element_type=f32)
        gg_ref[...] = lax.dot_general(cot_ref[...], wo_ref[...], NT, preferred_element_type=f32)

    @pl.when(i == 0)
    def _():
        if inside:
            wait = start_gather(L, count, *given, tok_ref, wts_ref, par_ref, halo_ref, *sems)

        def tile(r):
            normed_ref[pl.ds(r, RT), :] = norm(tok_ref[pl.ds(r, RT), :])

        row_tiles(T, tile)
        proj_ref[...] = jnp.zeros_like(proj_ref)
        dims = marks_ref.shape
        place = lax.broadcasted_iota(jnp.int32, dims, 0) + lax.axis_index("chan") * T
        lane = lax.broadcasted_iota(jnp.int32, dims, 1)
        reach = jnp.where(lane < K - 1, lane + 1, 1)
        found = jnp.zeros(dims, f32)
        start = jnp.int32(0)
        for k in range(len_ref.shape[1]):
            found = jnp.where((start > place - reach) & (start <= place), 1.0, found)
            start = start + len_ref[0, k]
        marks_ref[...] = jnp.where(lane < K - 1, 1.0 - found, found * CUT)
        products()
        if inside:
            wait()
            results[0][...] = wts_ref[...]
            results[1][...] = par_ref[...]
        lead_device = lax.axis_index("chan") == 0
        halo = jnp.where(lead_device, jnp.zeros(halo_ref.shape, f32), halo_ref[...].astype(f32))
        hn_ref[...] = norm(halo)

    pl.when(i > 0)(products)
    low = jnp.dot(hn_ref[...], wi_ref[...], preferred_element_type=f32).astype(bf16)
    inner_ref[0:HALO, :] = low
    xs_ref[0:HALO, :] = low.astype(f32)

    for k in range(sub):
        c = slice(k * EB, (k + 1) * EB)
        taps = [par_ref[first + k, L.conv + j : L.conv + j + 1, :] for j in range(K)]
        bias = par_ref[first + k, L.conv_b : L.conv_b + 1, :]

        def tile(r, c=c, taps=taps, bias=bias):
            rows = pl.ds(r, RT)
            block = xs_ref[pl.ds(pl.multiple_of(r + HALO - 8, 8), RT + 8), c]
            total = bias + taps[K - 1] * block[8:]
            for j in range(1, K):
                usable = marks_ref[rows, j - 1 : j]
                total = total + taps[K - 1 - j] * (block[8 - j : RT + 8 - j] * usable)
            act = total * jax.nn.sigmoid(total)
            cs_ref[rows, c] = total
            act_ref[rows, c] = act
            low_ref[rows, c] = act.astype(bf16)
            gate = gate_ref[rows, c]
            passed = gg_ref[rows, c] * (gate * jax.nn.sigmoid(gate))
            g_ref[rows, c] = passed.astype(bf16).astype(f32)

        row_tiles(T, tile)
        proj_ref[...] += lax.dot_general(low_ref[:, c], wts_ref[first + k], NT, preferred_element_type=f32)

    @pl.when(i == pl.num_programs(0) - 1)
    def _():
        turned = proj_ref[...].T
        for ref, start in ((bch_ref, L.R), (cch_ref, L.R + N)):
            for j in range(T // TC):
                ref[j] = turned[start : start + N, j * TC : (j + 1) * TC]


def front(L, count, lengths, tokens, gain, in_weight, out_weight, cot, parts, gathered):
    T, D = tokens.shape
    E = out_weight.shape[0]
    sub = 2
    wide = EB * sub
    steps = E // wide
    N = L.N
    inside = parts is not None
    more_out, scratch, options = [], [], {}
    if inside:
        given, given_specs = parts, [whole(*v.shape) for v in parts]
        more_out = [shape(bf16, count, WTS, EB), shape(f32, count, PAR, EB)]
        scratch = [pltpu.VMEM(o.shape, o.dtype) for o in more_out] + [pltpu.VMEM((HALO, D), bf16)]
        scratch += gather_scratch(count)
        options = dict(collective_id=1, has_side_effects=True)
    else:
        given, given_specs = gathered, [lead(WTS, EB, sub), lead(PAR, EB, sub), whole(HALO, D)]
    return pl.pallas_call(
        functools.partial(front_kernel, L, count, inside),
        grid=(steps,),
        in_specs=[
            pl.BlockSpec(memory_space=pltpu.SMEM),
            whole(T, D), whole(D), cols(D, wide), cols(D, wide, steps), tall(wide, D), whole(T, D),
        ] + given_specs,
        out_specs=[whole(T + 8, 8), whole(T, D), cols(T + HALO, wide)] + [cols(T, wide)] * 5 + [
            whole(T, 128), whole(T // TC, N, TC), whole(T // TC, N, TC),
        ] + [whole(*o.shape) for o in more_out],
        out_shape=[shape(f32, T + 8, 8), shape(bf16, T, D), shape(bf16, T + HALO, E)]
        + [shape(f32, T, E)] * 5
        + [shape(f32, T, 128), shape(f32, T // TC, N, TC), shape(f32, T // TC, N, TC)]
        + more_out,
        scratch_shapes=[
            pltpu.VMEM((HALO, D), bf16),
            pltpu.VMEM((T + HALO, wide), f32),
            pltpu.VMEM((T, wide), bf16),
        ] + scratch,
        compiler_params=params(**options),
        name="front",
    )(lengths, tokens, gain, in_weight, in_weight, out_weight, cot, *given)


def rates(L, par_ref):
    return -jnp.exp(par_ref[0, L.decay : L.decay + L.N, :]) * LOG2E


def lane_tiles(values):
    return [values[:, k * 128 : (k + 1) * 128] for k in range(EB // 128)]


def row_at(ref, t):
    return lane_tiles(ref[pl.ds(t, 1), :])


def spread(columns, j):
    return jnp.broadcast_to(columns[:, j : j + 1], (columns.shape[0], 128))


def ahead_of(steps, fetch):
    steps = list(steps)
    loaded = [fetch(j) for j in steps[:2]]
    for k, j in enumerate(steps):
        if k + 2 < len(steps):
            loaded.append(fetch(steps[k + 2]))
        yield j, loaded[k]


def softplus(x):
    return jnp.maximum(x, 0.0) + jnp.log1p(jnp.exp(-jnp.abs(x)))


def pre_kernel(
    L, count, proj_ref, par_ref, wts_ref, act_ref, g_ref, marks_ref, b_ref, c_ref,
    spre_ref, dtk_ref, u_ref, enter_ref, arrive_ref, ahead_ref, behind_ref, got_ref,
    send_sem, recv_sem,
):
    T, E = act_ref.shape[0], enter_ref.shape[1]
    N = L.N
    i = pl.program_id(0)
    blocks = E // EB
    si, ci = lax.axis_index("seq"), lax.axis_index("chan")

    @pl.when(i == 0)
    def _():
        barrier = pltpu.get_barrier_semaphore()
        for k in range(1, count):
            pl.semaphore_signal(
                barrier, inc=1, device_id=(si, lax.rem(ci + k, count)),
                device_id_type=pl.DeviceIdType.MESH,
            )
        pl.semaphore_wait(barrier, count - 1)

    low = proj_ref[:, 0 : L.R].astype(bf16)
    weights = wts_ref[0, L.step : L.step + L.R, :]
    bias = par_ref[0, L.step_b : L.step_b + 1, :]
    spre_ref[...] = jnp.dot(low, weights, preferred_element_type=f32) + bias

    def tile(r):
        rows = pl.ds(r, RT)
        step = softplus(spre_ref[rows, :])
        u_ref[rows, :] = step * act_ref[rows, :]
        dtk_ref[rows, :] = step + marks_ref[rows, 3:4]

    row_tiles(T, tile)
    rate = lane_tiles(rates(L, par_ref))
    tiles = len(rate)

    def chunk(c, carry):
        h, through, head = (list(carry[k * tiles : (k + 1) * tiles]) for k in range(3))
        base = pl.multiple_of(c * TC, TC)
        b_cols, c_cols = b_ref[c], c_ref[c]

        def fetch(j):
            rows = [row_at(ref, base + j) for ref in (dtk_ref, u_ref, g_ref)]
            return rows + [spread(b_cols, j), spread(c_cols, j)]

        for j, (d, u, g, b_now, c_now) in ahead_of(range(TC), fetch):
            for k in range(tiles):
                factor = jnp.exp2(d[k] * rate[k])
                h[k] = factor * h[k] + b_now * u[k]
                through[k] = factor * through[k]
                head[k] = head[k] + through[k] * (c_now * g[k])
        return tuple(h + through + head)

    zero = jnp.zeros((N, 128), f32)
    out = lax.fori_loop(0, T // TC, chunk, (zero,) * tiles + (zero + 1.0,) * tiles + (zero,) * tiles)
    h, through, head = (jnp.concatenate(out[k * tiles : (k + 1) * tiles], axis=1) for k in range(3))
    zero = jnp.zeros((N, EB), f32)
    ahead_ref[i, 0:N, :] = h
    ahead_ref[i, N:, :] = through
    behind_ref[i, 0:N, :] = head
    behind_ref[i, N:, :] = through

    def send(b, k, forward):
        return pltpu.make_async_remote_copy(
            src_ref=(ahead_ref if forward else behind_ref).at[b], dst_ref=got_ref.at[count - k, b],
            send_sem=send_sem.at[k, b], recv_sem=recv_sem.at[count - k, b],
            device_id=(si, lax.rem(ci + k, count)), device_id_type=pl.DeviceIdType.MESH,
        )

    for k in range(1, count):
        @pl.when(ci + k < count)
        def _(k=k):
            send(i, k, True).start()

        @pl.when(ci + k >= count)
        def _(k=k):
            send(i, k, False).start()

    @pl.when(i == blocks - 1)
    def _():
        for b in range(blocks):
            for k in range(1, count):
                send(b, k, True).wait()
        for b in range(blocks):
            span = slice(b * EB, (b + 1) * EB)
            entering, arriving = zero, zero
            for k in range(1, count):
                before = ci + k >= count
                got = got_ref[k, b]
                entering = jnp.where(before, got[0:N] + got[N:] * entering, entering)
            for k in range(count - 1, 0, -1):
                behind = ci + k < count
                got = got_ref[k, b]
                arriving = jnp.where(behind, got[0:N] + got[N:] * arriving, arriving)
            enter_ref[:, span] = entering
            arrive_ref[:, span] = arriving


def pre_scan(L, count, proj, par, wts, act, g, marks, b_cols, c_cols):
    T, E = act.shape
    N = L.N
    blocks = E // EB
    state = shape(f32, N, E)
    return pl.pallas_call(
        functools.partial(pre_kernel, L, count),
        grid=(blocks,),
        in_specs=[
            whole(T, 128), lead(PAR, EB), lead(WTS, EB), cols(T), cols(T), whole(*marks.shape),
            once(*b_cols.shape), once(*c_cols.shape),
        ],
        out_specs=[cols(T)] * 3 + [whole(N, E)] * 2,
        out_shape=[shape(f32, T, E)] * 3 + [state] * 2,
        scratch_shapes=[
            pltpu.VMEM((blocks, 2 * N, EB), f32),
            pltpu.VMEM((blocks, 2 * N, EB), f32),
            pltpu.VMEM((count, blocks, 2 * N, EB), f32),
            pltpu.SemaphoreType.DMA((count, blocks)),
            pltpu.SemaphoreType.DMA((count, blocks)),
        ],
        compiler_params=params(collective_id=2, has_side_effects=True),
        name="pre_scan",
    )(proj, par, wts, act, g, marks, b_cols, c_cols)


def fold_rows(refs, r):
    sums = []
    for ref in refs:
        parts = [ref[pl.ds(r * 8 + k, 8, stride=8), :] for k in range(8)]
        while len(parts) > 1:
            parts = [x + y for x, y in zip(parts[::2], parts[1::2])]
        sums.append(parts[0])
    return jnp.concatenate(sums, axis=1)


def halves(values):
    return values[0:8] + values[8:16]


def lane_sums(states, acc_ref, out_ref, chunks):
    width = TC * states
    ones = jnp.ones((TC, 128), bf16)
    group = chunks // 4
    for k in range(4):
        part = acc_ref[k * group * width : (k + 1) * group * width, :].astype(bf16)
        sums = lax.dot_general(ones, part, NT, preferred_element_type=f32)
        for c in range(group):
            row = (k * group + c) * TC
            out_ref[row : row + TC, :] = sums[:, c * width : (c + 1) * width]


def fwd_kernel(
    L, dtk_ref, u_ref, b_ref, c_ref, g_ref, par_ref, hin_ref, act_ref, gate_ref, gg_ref,
    wo_ref, cot_ref, tok_ref, normed_ref, wg_ref,
    h_ref, gc_ref, block_ref, gout_ref, gin_ref, gn_ref,
    acc_ref, gated_ref, ggate_ref, branch_ref, *y_refs,
):
    rate = lane_tiles(rates(L, par_ref))
    T, states = u_ref.shape[0], L.N
    chunks = T // TC
    width = TC * states
    i = pl.program_id(0)

    @pl.when(i == 0)
    def _():
        acc_ref[...] = jnp.zeros_like(acc_ref)
        gn_ref[...] = jnp.zeros_like(gn_ref)
        branch_ref[...] = jnp.zeros_like(branch_ref)

    h_ref[0:states, :] = hin_ref[...].astype(bf16)

    def chunk(c, carry):
        h = list(carry)
        base = pl.multiple_of(c * TC, TC)
        row = pl.multiple_of(c * width, width)
        b_cols, c_cols = b_ref[c], c_ref[c]

        def fetch(j):
            at = pl.ds(row + j * states, states)
            rows = [row_at(ref, base + j) for ref in (dtk_ref, u_ref, g_ref)]
            return rows + [spread(b_cols, j), spread(c_cols, j), acc_ref[at, :]]

        for j, (d, u, g, b_now, c_now, acc) in ahead_of(range(TC), fetch):
            for k in range(len(h)):
                h[k] = jnp.exp2(d[k] * rate[k]) * h[k] + b_now * u[k]
                h_ref[pl.ds(row + (j + 1) * states, states), k * 128 : (k + 1) * 128] = h[k].astype(bf16)
                y_refs[k][pl.ds((base + j) * 8, 8), :] = halves(c_now * h[k])
                acc = acc + h[k] * g[k]
            acc_ref[pl.ds(row + j * states, states), :] = acc
        return tuple(h)

    lax.fori_loop(0, chunks, chunk, tuple(lane_tiles(hin_ref[...])))
    skip = par_ref[0, L.skip : L.skip + 1, :]

    def tile(k, unused):
        rows = pl.ds(pl.multiple_of(k * 16, 16), 16)
        y = jnp.concatenate([fold_rows(y_refs, k * 16), fold_rows(y_refs, k * 16 + 8)], axis=0)
        mixer = (y + skip * act_ref[rows, :]).astype(bf16).astype(f32)
        gate = gate_ref[rows, :]
        sig = jax.nn.sigmoid(gate)
        gated_ref[rows, :] = (mixer * (gate * sig)).astype(bf16)
        ggate_ref[rows, :] = (gg_ref[rows, :] * mixer * sig * (1.0 + gate * (1.0 - sig))).astype(bf16)
        return unused

    lax.fori_loop(0, T // 16, tile, 0)
    branch_ref[...] += jnp.dot(gated_ref[...], wo_ref[...], preferred_element_type=f32)
    gout_ref[...] = lax.dot_general(
        gated_ref[...], cot_ref[...], TN, preferred_element_type=f32
    ).astype(bf16)
    gin_ref[...] = lax.dot_general(
        ggate_ref[...], normed_ref[...], TN, preferred_element_type=f32
    ).astype(bf16)
    gn_ref[...] += lax.dot_general(ggate_ref[...], wg_ref[...], NT, preferred_element_type=f32)

    @pl.when(i == pl.num_programs(0) - 1)
    def _():
        block_ref[...] = (tok_ref[...].astype(f32) + branch_ref[...]).astype(bf16)
        lane_sums(states, acc_ref, gc_ref, chunks)


def fwd_scan(L, dtk, u, b_cols, c_cols, g, par, entering, act, gate, gg, out_weight, cot, tokens, normed, in_weight):
    T, E = dtk.shape
    D = tokens.shape[1]
    N = L.N
    rows = (T + 1) * N
    blocks = E // EB
    return pl.pallas_call(
        functools.partial(fwd_kernel, L),
        grid=(blocks,),
        in_specs=[
            cols(T), cols(T), once(*b_cols.shape), once(*c_cols.shape), cols(T), lead(PAR, EB), cols(N),
            cols(T), cols(T), cols(T), tall(EB, D), whole(T, D), whole(T, D), whole(T, D),
            cols(D, EB, blocks),
        ],
        out_specs=[
            cols(rows), whole(T, TC * N), whole(T, D), tall(EB, D), tall(EB, D), whole(T, D),
        ],
        out_shape=[
            shape(bf16, rows, E), shape(f32, T, TC * N), shape(bf16, T, D), shape(bf16, E, D),
            shape(bf16, E, D), shape(f32, T, D),
        ],
        scratch_shapes=[
            pltpu.VMEM((T * N, 128), f32), pltpu.VMEM((T, EB), bf16), pltpu.VMEM((T, EB), bf16),
            pltpu.VMEM((T, D), f32),
        ] + [pltpu.VMEM((T * 8, 128), f32)] * (EB // 128),
        compiler_params=params(),
        name="fwd_scan",
    )(dtk, u, b_cols, c_cols, g, par, entering, act, gate, gg, out_weight, cot, tokens, normed, in_weight)


def bwd_kernel(
    L, sums, blocks, dtk_ref, u_ref, g_ref, b_ref, c_ref, par_ref, wts_ref, fin_ref, h_ref, spre_ref, act_ref, proj_ref,
    gc_ref, *refs,
):
    arrays = len(sums.kinds)
    x_refs, refs = refs[:arrays], refs[arrays:]
    gap_ref, chan_ref, gproj_ref = refs[:3]
    o_refs, refs = refs[3 : 3 + arrays], refs[3 + arrays :]
    acc_ref, gb_ref, rank_ref, pre_ref = refs[:4]
    rate = lane_tiles(rates(L, par_ref))
    tiles = len(rate)
    bsum_refs, wsum_refs = refs[4 : 4 + tiles], refs[4 + tiles : 4 + 2 * tiles]
    sums.bind(x_refs, o_refs, refs[4 + 2 * tiles :])
    T, states = u_ref.shape[0], L.N
    chunks = T // TC
    width = TC * states
    i = pl.program_id(0)

    @pl.when(i == 0)
    def _():
        acc_ref[...] = jnp.zeros_like(acc_ref)
        rank_ref[...] = jnp.zeros_like(rank_ref)
        sums.barrier()

    def chunk(i, carry):
        flow, total = list(carry[:tiles]), list(carry[tiles:])
        c = chunks - 1 - i
        base = pl.multiple_of(c * TC, TC)
        row = pl.multiple_of(c * width, width)
        b_cols, c_cols = b_ref[c], c_ref[c]

        def fetch(j):
            at = pl.ds(row + j * states, states)
            rows = [row_at(ref, base + j) for ref in (dtk_ref, u_ref, g_ref)]
            return rows + [spread(b_cols, j), spread(c_cols, j), acc_ref[at, :], lane_tiles(h_ref[at, :])]

        for j, (d, u, g, b_now, c_now, acc, before) in ahead_of(reversed(range(TC)), fetch):
            part = pl.ds((base + j) * 8, 8)
            for k in range(tiles):
                adj = c_now * g[k] + flow[k]
                flow[k] = jnp.exp2(d[k] * rate[k]) * adj
                wr = flow[k] * before[k].astype(f32) * rate[k]
                total[k] = total[k] + wr * d[k]
                wsum_refs[k][part, :] = halves(wr)
                bsum_refs[k][part, :] = halves(adj * b_now)
                acc = acc + adj * u[k]
            acc_ref[pl.ds(row + j * states, states), :] = acc
        return tuple(flow) + tuple(total)

    none = jnp.zeros((states, 128), f32)
    out = tuple(lane_tiles(fin_ref[...])) + (none,) * tiles
    for q in range(BLOCK_SLOTS):
        for n in range(sums.ticks()):
            block, quarter = divmod(n, BLOCK_SLOTS)
            if quarter == q and block < blocks:
                pl.when(i == block)(functools.partial(sums.tick, n))
        out = lax.fori_loop(q * chunks // BLOCK_SLOTS, (q + 1) * chunks // BLOCK_SLOTS, chunk, out)
    total = jnp.concatenate(out[tiles:], axis=1)
    skip = par_ref[0, L.skip : L.skip + 1, :]

    def tile(k, carry):
        bias_sum, skip_sum = carry
        rows = pl.ds(pl.multiple_of(k * 16, 16), 16)
        bsum, wsum = (
            jnp.concatenate([fold_rows(refs, k * 16), fold_rows(refs, k * 16 + 8)], axis=0)
            for refs in (bsum_refs, wsum_refs)
        )
        spre, act, g = spre_ref[rows, :], act_ref[rows, :], g_ref[rows, :]
        grad = (wsum * (1.0 / LOG2E) + act * bsum) * jax.nn.sigmoid(spre)
        gap_ref[rows, :] = g * skip + softplus(spre) * bsum
        pre_ref[rows, :] = grad.astype(bf16)
        bias_sum = bias_sum + halves(grad)
        skip_sum = skip_sum + halves(g * act)
        return bias_sum, skip_sum

    none = jnp.zeros((8, EB), f32)
    bias_sum, skip_sum = lax.fori_loop(0, T // 16, tile, (none, none))
    R = L.R
    pre = pre_ref[...]
    step_low = proj_ref[...].astype(bf16)
    grad_step_w = lax.dot_general(step_low, pre, TN, preferred_element_type=f32)
    chan_ref[0] = jnp.concatenate(
        [
            grad_step_w[0:R],
            total * (1.0 / LOG2E),
            jnp.sum(bias_sum, axis=0, keepdims=True),
            jnp.sum(skip_sum, axis=0, keepdims=True),
            jnp.zeros((128 - R - states - 2, EB), f32),
        ],
        axis=0,
    ).astype(bf16)
    weights = wts_ref[0, L.step : L.step + R, :].astype(f32)
    weights = jnp.concatenate([weights, jnp.zeros((128 - R, EB), f32)], axis=0).astype(bf16)
    rank_ref[...] += lax.dot_general(pre, weights, NT, preferred_element_type=f32)

    @pl.when(i == pl.num_programs(0) - 1)
    def _():
        lane_sums(states, acc_ref, gb_ref, chunks)
        dims = (width, 128)
        state = lax.rem(lax.broadcasted_iota(jnp.int32, dims, 0), states)
        target = lax.broadcasted_iota(jnp.int32, dims, 1)
        diag = same_step(states, T)
        total = rank_ref[...]
        for ref, start in ((gb_ref, R), (gc_ref, R + states)):
            fold = (target == state + start).astype(f32)
            kept = jnp.where(diag, ref[...], 0.0)
            total = total + jnp.dot(
                kept, fold, precision=lax.Precision.HIGHEST, preferred_element_type=f32
            )
        gproj_ref[...] = total.astype(bf16)
        for n in range(blocks * BLOCK_SLOTS, sums.ticks()):
            sums.tick(n)
        sums.drain()


def bwd_scan(L, dtk, u, g, b_cols, c_cols, par, wts, arriving, held, spre, act, proj, grad_c, arrays, sums):
    T, E = dtk.shape
    N = L.N
    blocks = E // EB
    return pl.pallas_call(
        functools.partial(bwd_kernel, L, sums, blocks),
        grid=(blocks,),
        in_specs=[
            cols(T), cols(T), cols(T), once(*b_cols.shape), once(*c_cols.shape), lead(PAR, EB),
            lead(WTS, EB), cols(N), cols(held.shape[0]), cols(T), cols(T), whole(T, 128), whole(T, TC * N),
        ] + [once(*v.shape) for v in arrays],
        out_specs=[cols(T), lead(128, EB), whole(T, 128)] + [whole(*o.shape) for o in sums.outs()],
        out_shape=[shape(f32, T, E), shape(bf16, blocks, 128, EB), shape(bf16, T, 128)] + sums.outs(),
        scratch_shapes=[
            pltpu.VMEM((T * N, 128), f32),
            pltpu.VMEM((T, TC * N), f32), pltpu.VMEM((T, 128), f32), pltpu.VMEM((T, EB), bf16),
        ] + [pltpu.VMEM((T * 8, 128), f32)] * (2 * EB // 128) + sums.scratch(),
        compiler_params=params(collective_id=3, has_side_effects=True),
        name="bwd_scan",
    )(dtk, u, g, b_cols, c_cols, par, wts, arriving, held, spre, act, proj, grad_c, *arrays)


def conv_kernel(
    L, count, gap_ref, gproj_ref, wts_ref, act_ref, cs_ref, inner_ref, marks_ref,
    gc_ref, chan_ref, after_ref, xs_ref, edge_ref, got_ref, send_sem, recv_sem,
):
    T = gap_ref.shape[0]
    i = pl.program_id(0)
    blocks = edge_ref.shape[0]
    si, ci = lax.axis_index("seq"), lax.axis_index("chan")
    before = lax.rem(ci + count - 1, count)

    @pl.when(i == 0)
    def _():
        barrier = pltpu.get_barrier_semaphore()
        for other in (before, lax.rem(ci + 1, count)):
            pl.semaphore_signal(barrier, inc=1, device_id=(si, other), device_id_type=pl.DeviceIdType.MESH)
        pl.semaphore_wait(barrier, 2)

    def edge(b):
        return pltpu.make_async_remote_copy(
            src_ref=edge_ref.at[b], dst_ref=got_ref.at[b], send_sem=send_sem.at[b], recv_sem=recv_sem.at[b],
            device_id=(si, before), device_id_type=pl.DeviceIdType.MESH,
        )

    K, wide = L.K, L.R + 2 * L.N
    weights = wts_ref[0].astype(f32)
    row = lax.broadcasted_iota(jnp.int32, weights.shape, 0)
    weights = jnp.where(row < wide, weights, 0.0).astype(bf16)
    gc_ref[...] = jnp.dot(gproj_ref[...], weights, preferred_element_type=f32)
    act_low = act_ref[...].astype(bf16)
    grad_proj = lax.dot_general(gproj_ref[...], act_low, TN, preferred_element_type=f32)
    xs_ref[...] = inner_ref[...].astype(f32)

    def tile(k, carry):
        r = pl.multiple_of(k * RT, RT)
        rows = pl.ds(r, RT)
        total = cs_ref[rows, :]
        sig = jax.nn.sigmoid(total)
        grad = (gc_ref[rows, :] + gap_ref[rows, :]) * sig * (1.0 + total * (1.0 - sig))
        gc_ref[rows, :] = grad
        block = xs_ref[pl.ds(pl.multiple_of(r + HALO - 8, 8), RT + 8), :]
        out = [carry[K] + jnp.sum(grad.reshape(RT // 8, 8, EB), axis=0)]
        for j in range(K):
            part = grad * block[8 - j : RT + 8 - j]
            if j > 0:
                part = part * marks_ref[rows, j - 1 : j]
            out.insert(0, carry[K - 1 - j] + jnp.sum(part.reshape(RT // 8, 8, EB), axis=0))
        return tuple(out)

    none = jnp.zeros((8, EB), f32)
    sums = lax.fori_loop(0, T // RT, tile, (none,) * (K + 1))
    edge_ref[i] = gc_ref[0:8, :]
    edge(i).start()
    chan_ref[0] = jnp.concatenate(
        [grad_proj[0:wide]]
        + [jnp.sum(s, axis=0, keepdims=True) for s in sums]
        + [jnp.zeros((128 - wide - K - 1, EB), f32)],
        axis=0,
    ).astype(bf16)

    @pl.when(i == blocks - 1)
    def _():
        for b in range(blocks):
            edge(b).wait()
            rows = jnp.where(ci == count - 1, 0.0, got_ref[b])
            after_ref[:, b * EB : (b + 1) * EB] = rows


def conv_back(L, count, gap, gproj, wts, act, cs, inner, marks):
    T, E = gap.shape
    blocks = E // EB
    return pl.pallas_call(
        functools.partial(conv_kernel, L, count),
        grid=(blocks,),
        in_specs=[
            cols(T), whole(T, 128), lead(WTS, EB), cols(T), cols(T), cols(T + HALO), whole(*marks.shape),
        ],
        out_specs=[cols(T), lead(128, EB), whole(8, E)],
        out_shape=[shape(f32, T, E), shape(bf16, blocks, 128, EB), shape(f32, 8, E)],
        scratch_shapes=[
            pltpu.VMEM((T + HALO, EB), f32),
            pltpu.VMEM((blocks, 8, EB), f32),
            pltpu.VMEM((blocks, 8, EB), f32),
            pltpu.SemaphoreType.DMA((blocks,)),
            pltpu.SemaphoreType.DMA((blocks,)),
        ],
        compiler_params=params(collective_id=4, has_side_effects=True),
        name="conv_back",
    )(gap, gproj, wts, act, cs, inner, marks)


def tail_kernel(
    L, gc_ref, after_ref, par_ref, marks_ref, normed_ref, wi_ref, gn_ref, tok_ref, cot_ref, gain_ref,
    gin_ref, gtok_ref, ggain_ref, ext_ref, low_ref, sum_ref,
):
    T, D = tok_ref.shape
    K = L.K
    i = pl.program_id(0)
    ext_ref[0:T, :] = gc_ref[...]
    ext_ref[T : T + 8, :] = after_ref[...]
    taps = [par_ref[0, L.conv + j : L.conv + j + 1, :] for j in range(K)]

    def tile(r):
        block = ext_ref[pl.ds(r, RT + 8), :]
        marks = marks_ref[pl.ds(r, RT + 8), :]
        total = taps[K - 1] * block[0:RT]
        for j in range(1, K):
            masked = block * marks[:, j - 1 : j]
            total = total + taps[K - 1 - j] * masked[j : RT + j]
        low_ref[pl.ds(r, RT), :] = total.astype(bf16)

    row_tiles(T, tile)
    gin_ref[...] = lax.dot_general(
        low_ref[...], normed_ref[...], TN, preferred_element_type=f32
    ).astype(bf16)
    part = lax.dot_general(low_ref[...], wi_ref[...], NT, preferred_element_type=f32)

    @pl.when(i == 0)
    def _():
        sum_ref[...] = gn_ref[...] + part

    @pl.when(i > 0)
    def _():
        sum_ref[...] += part

    @pl.when(i == pl.num_programs(0) - 1)
    def _():
        gain = gain_ref[...].reshape(1, D)

        def last(k, total):
            rows = pl.ds(pl.multiple_of(k * 16, 16), 16)
            x = tok_ref[rows, :].astype(f32)
            grad = sum_ref[rows, :]
            inv = lax.rsqrt(jnp.mean(x * x, axis=1, keepdims=True) + epsilon)
            scaled = grad * gain
            mean = jnp.mean(x * scaled, axis=1, keepdims=True)
            gtok_ref[rows, :] = (
                cot_ref[rows, :].astype(f32) + inv * scaled - x * (inv * inv * inv * mean)
            )
            return total + jnp.sum((grad * x * inv).reshape(2, 8, D), axis=0)

        total = lax.fori_loop(0, T // 16, last, jnp.zeros((8, D), f32))
        ggain_ref[...] = jnp.sum(total, axis=0, keepdims=True)


def tail(L, gc, after, par, marks, normed, in_weight, gn, tokens, cot, gain):
    T, E = gc.shape
    D = tokens.shape[1]
    blocks = E // EB
    return pl.pallas_call(
        functools.partial(tail_kernel, L),
        grid=(blocks,),
        in_specs=[
            cols(T), cols(8), lead(PAR, EB), whole(*marks.shape), whole(T, D), cols(D), whole(T, D),
            whole(T, D), whole(T, D), whole(D),
        ],
        out_specs=[tall(EB, D), whole(T, D), whole(1, D)],
        out_shape=[shape(bf16, E, D), shape(f32, T, D), shape(f32, 1, D)],
        scratch_shapes=[
            pltpu.VMEM((T + 8, EB), f32), pltpu.VMEM((T, EB), bf16), pltpu.VMEM((T, D), f32),
        ],
        compiler_params=params(),
        name="tail",
    )(gc, after, par, marks, normed, in_weight, gn, tokens, cot, gain)


class Sums:
    def __init__(self, chan_count, seq_count, kinds, shapes, phases, skew=1, pace=1):
        self.cc, self.sc = chan_count, seq_count
        self.kinds = kinds
        self.phases, self.skew, self.pace = phases, skew, pace
        self.size = 8 * seq_count
        self.bits = [1 << i for i in range(chan_count.bit_length() - 1)]
        self.z_bits = [2 << i for i in range(seq_count.bit_length() - 2)]
        self.pieces = [
            (a, r, dims[2]) for a, dims in enumerate(shapes) for r in range(0, dims[1], 2 * self.size)
        ]
        self.shapes = shapes

    def half(self, p):
        return self.kinds[self.pieces[p][0]] is not None

    def stages(self, p):
        bits = self.bits if p % 2 == 0 else self.bits[::-1]
        return (
            [("core", 1)] + [("chan", b) for b in bits] + [("z", b) for b in self.z_bits]
            + [("zgather", b) for b in self.z_bits[::-1]] + ([("move", 0)] if self.half(p) else [])
            + [("cgather", 1)]
        )

    def span(self, p):
        halvings = 1 + len(self.bits) + len(self.z_bits)
        phase = self.phases[self.pieces[p][0]]
        first = halvings if phase == "gather" else 0
        return first, halvings if phase == "halve" else len(self.stages(p))

    def begin(self, p):
        phase = self.phases[self.pieces[p][0]]
        before = [q for q in range(p) if self.phases[self.pieces[q][0]] == phase]
        return self.skew * (len(before) // 2)

    def ticks(self):
        return max(
            self.begin(p) + self.pace * (self.span(p)[1] - self.span(p)[0]) for p in range(len(self.pieces))
        ) + 1

    def final(self, p):
        a, first, width = self.pieces[p]
        return pl.ds(first // (2 * self.size) * 16, 16)

    def outs(self):
        found = []
        for kind, dims, phase in zip(self.kinds, self.shapes, self.phases):
            if phase == "halve":
                found.append(shape(bf16, dims[1] // (2 * self.size) * 16, dims[2]))
            else:
                found.append(shape(bf16, *(dims[1:] if kind is None else (2,) + tuple(dims[1:]))))
        return found

    def scratch(self):
        found = []
        for p, (a, r, width) in enumerate(self.pieces):
            small = self.span(p)[0] > 0
            for k in range(len(self.bits) + 1):
                dims = (self.cc >> k, self.size, width)
                found.append(pltpu.VMEM((1, 16, 128) if small else dims, bf16))
            for k in range(len(self.z_bits)):
                dims = (self.size >> (k + 1), width)
                found.append(pltpu.VMEM((16, 128) if small else dims, bf16))
            found.append(pltpu.VMEM((self.size, width), bf16))
        dims = (len(self.pieces), len(self.bits) + 2 * len(self.z_bits) + 3, max(2, self.cc // 2))
        return found + [pltpu.SemaphoreType.DMA(dims), pltpu.SemaphoreType.DMA(dims)]

    def bind(self, x_refs, o_refs, scratch):
        self.x, self.o = x_refs, o_refs
        each = len(self.bits) + len(self.z_bits) + 2
        self.held = [scratch[p * each : (p + 1) * each] for p in range(len(self.pieces))]
        self.send_sem, self.recv_sem = scratch[-2:]
        self.si, self.ci = lax.axis_index("seq"), lax.axis_index("chan")
        self.core = lax.rem(self.si, 2)

    def side(self, bit):
        return lax.rem(self.si // bit, 2)

    def across(self, bit):
        return (self.si + bit - 2 * bit * self.side(bit), self.ci)

    def barrier(self):
        barrier = pltpu.get_barrier_semaphore()
        others = [(self.si, lax.rem(self.ci + k, self.cc)) for k in range(1, self.cc)]
        others += [self.across(bit) for bit in [1] + self.z_bits]
        for other in others:
            pl.semaphore_signal(barrier, inc=1, device_id=other, device_id_type=pl.DeviceIdType.MESH)
        pl.semaphore_wait(barrier, len(others))

    def copy(self, p, s, slot, src, dst, device):
        return pltpu.make_async_remote_copy(
            src_ref=src, dst_ref=dst, send_sem=self.send_sem.at[p, s, slot],
            recv_sem=self.recv_sem.at[p, s, slot], device_id=device, device_id_type=pl.DeviceIdType.MESH,
        )

    def kept(self, p, s, keep):
        name, bit = self.stages(p)[s]
        if name == "core":
            a, start, width = self.pieces[p]
            side = self.core if keep else 1 - self.core
            return [self.x[a].at[:, pl.ds(pl.multiple_of(start + side * self.size, 16), self.size), :]]
        ref = self.held[p][s - 1]
        if name == "z":
            side = self.side(bit) if keep else 1 - self.side(bit)
            k = self.z_bits.index(bit)
            rows = self.size >> (k + 1)
            rows = pl.ds(pl.multiple_of(side * rows, 16), rows)
            return [ref.at[0, rows, :] if k == 0 else ref.at[rows, :]]
        mine = lax.rem(self.ci // bit, 2)
        side = mine if keep else 1 - mine
        left = sorted(b for n, b in self.stages(p)[s : 1 + len(self.bits)])
        low = 1 << left.index(bit)
        return [
            ref.at[pl.ds((i // low) * 2 * low + side * low + i % low, 1)]
            for i in range((1 << len(left)) // 2)
        ]

    def landing(self, p, s):
        dst = self.held[p][s]
        return [dst.at[pl.ds(i, 1)] for i in range(dst.shape[0])] if self.stages(p)[s][0] == "chan" else [dst]

    def gathered(self, p, done):
        start, rows = 0, self.size
        for bit in self.z_bits[:done]:
            rows //= 2
            start = start + self.side(bit) * rows
        if self.half(p):
            return self.held[p][-1].at[pl.ds(pl.multiple_of(start, 16), rows), :]
        start = start + self.pieces[p][1] + self.core * self.size
        return self.o[self.pieces[p][0]].at[pl.ds(pl.multiple_of(start, 16), rows), :]

    def places(self, p):
        a, first, width = self.pieces[p]
        rows = pl.ds(pl.multiple_of(first + self.core * self.size, 16), self.size)
        return [self.o[a].at[b, rows, :] for b in range(2)] if self.half(p) else [self.o[a].at[rows, :]]

    def move(self, p, s, v):
        goal = self.kinds[self.pieces[p][0]] + v // 2
        place = self.places(p)[v % 2]
        return goal, place, self.copy(p, s, v % 2, self.held[p][-1], place, (self.si, goal))

    def copies(self, p, s):
        name, bit = self.stages(p)[s]
        if name in ("core", "chan", "z"):
            device = (self.si, self.ci + bit - 2 * bit * lax.rem(self.ci // bit, 2))
            device = device if name == "chan" else self.across(bit)
            pairs = zip(self.kept(p, s, False), self.landing(p, s))
            return [self.copy(p, s, i, src, dst, device) for i, (src, dst) in enumerate(pairs)]
        places = self.places(p)
        if name == "zgather":
            places = [self.gathered(p, self.z_bits.index(bit) + 1)]
        return [self.copy(p, s, b, place, place, self.across(bit)) for b, place in enumerate(places)]

    def taking_part(self, p, s, work):
        if self.half(p) and self.stages(p)[s][0] == "cgather":
            base = self.kinds[self.pieces[p][0]]
            pl.when((self.ci >= base) & (self.ci < base + self.cc // 2))(work)
        else:
            work()

    def start(self, p, s):
        if self.stages(p)[s][0] == "move":
            for v in range(self.cc):
                @pl.when(self.ci == v)
                def _(v=v):
                    goal, place, copy = self.move(p, s, v)
                    if goal == v:
                        place[...] = self.held[p][-1][...]
                    else:
                        copy.start()
            return

        def work():
            for copy in self.copies(p, s):
                copy.start()

        self.taking_part(p, s, work)

    def finish(self, p, s):
        name, bit = self.stages(p)[s]
        if name == "move":
            for v in range(self.cc):
                goal, place, copy = self.move(p, s, v)
                if goal != v:
                    pl.when(self.ci == goal)(copy.wait_recv)
            return

        def work():
            for copy in self.copies(p, s):
                copy.wait_recv()

        self.taking_part(p, s, work)
        if name in ("core", "chan", "z"):
            last = s == len(self.bits) + len(self.z_bits)
            for src, dst in zip(self.kept(p, s, True), self.landing(p, s)):
                total = (dst[...].astype(f32) + src[...].astype(f32)).astype(bf16)
                if last and self.span(p)[1] == s + 1:
                    dst = self.o[self.pieces[p][0]].at[self.final(p), :]
                elif last:
                    dst = self.gathered(p, len(self.z_bits))
                dst[...] = total

    def tick(self, n):
        for p in range(len(self.pieces)):
            first, end = self.span(p)
            s, rest = divmod(n - self.begin(p), self.pace)
            s += first
            if rest != 0:
                continue
            if first + 1 <= s <= end:
                self.finish(p, s - 1)
            if first > 0 and s == first:
                self.gathered(p, len(self.z_bits))[...] = self.x[self.pieces[p][0]][self.final(p), :]
            if first <= s < end:
                self.start(p, s)

    def drain(self):
        for p in range(len(self.pieces)):
            for s in range(*self.span(p)):
                if self.stages(p)[s][0] == "move":
                    for v in range(self.cc):
                        goal, place, copy = self.move(p, s, v)
                        if goal != v:
                            pl.when(self.ci == v)(copy.wait_send)
                    continue

                def work(p=p, s=s):
                    for copy in self.copies(p, s):
                        copy.wait_send()

                self.taking_part(p, s, work)


def sum_kernel(sums, *refs):
    arrays = len(sums.kinds)
    sums.bind(refs[:arrays], refs[arrays : 2 * arrays], refs[2 * arrays :])
    sums.barrier()
    for n in range(sums.ticks()):
        sums.tick(n)
    sums.drain()


def sum_owned(arrays, shapes, kinds, phases, chan_count, seq_count):
    sums = Sums(chan_count, seq_count, kinds, shapes, phases)
    vmem = pl.BlockSpec(memory_space=pltpu.VMEM)
    return pl.pallas_call(
        functools.partial(sum_kernel, sums),
        in_specs=[vmem] * len(arrays),
        out_specs=[vmem] * len(arrays),
        out_shape=sums.outs(),
        scratch_shapes=sums.scratch(),
        compiler_params=params(collective_id=0, has_side_effects=True),
        name="sum_owned",
    )(*arrays)


def unpack_kernel(L, inner_ref, gate_ref, out_ref, d_ref, e_ref, gin_ref, gout_ref, *refs):
    first = lax.axis_index("chan") < lax.axis_size("chan") // 2

    @pl.when(first)
    def _():
        gin_ref[...] = inner_ref[...].astype(f32).T

    @pl.when(jnp.logical_not(first))
    def _():
        gin_ref[...] = gate_ref[...].astype(f32).T

    gout_ref[...] = out_ref[...].astype(f32)
    d, e = d_ref[...].astype(f32), e_ref[...].astype(f32)
    R, N, K = L.R, L.N, L.K
    wide = R + 2 * N
    conv_w, conv_b, proj, step_w, step_b, decay, skip, gain = refs
    width = d.shape[1]
    step_w[...] = d[0:R]
    decay[...] = d[R : R + N]
    step_b[...] = d[R + N].reshape(width)
    skip[...] = d[R + N + 1].reshape(width)
    proj[...] = e[0:wide]
    conv_w[...] = e[wide : wide + K]
    conv_b[...] = e[wide + K].reshape(width)
    gain[...] = e[wide + K + 1].reshape(width)


def unpack(L, sums):
    width = sums[3].shape[1]
    rows, D = sums[0].shape
    R, N, K = L.R, L.N, L.K
    return pl.pallas_call(
        functools.partial(unpack_kernel, L),
        out_shape=[
            shape(f32, D, rows), shape(f32, *sums[2].shape), shape(f32, K, width), shape(f32, width),
            shape(f32, R + 2 * N, width), shape(f32, R, width), shape(f32, width),
            shape(f32, N, width), shape(f32, width), shape(f32, width),
        ],
        compiler_params=params(),
        name="unpack",
    )(*sums)


def local(
    tokens, norm_gain, in_weight, conv_weight, conv_bias, proj_weight, step_weight,
    step_bias, decay_log, skip_gain, out_weight, cotangent, lengths,
):
    T, D = tokens.shape
    E = in_weight.shape[1] // 2
    L = Layout(step_weight.shape[0], decay_log.shape[0], conv_weight.shape[0])
    ci = lax.axis_index("chan")
    cc = lax.axis_size("chan")
    sc = lax.axis_size("seq")
    blocks, share = E // EB, E // cc

    parts = (conv_weight, conv_bias, proj_weight.T, step_weight, step_bias, decay_log, skip_gain)
    gathered = None
    if share != EB:
        wts, par, halo = gather_params(L, cc, parts, tokens)

        def by_block(values):
            values = jnp.moveaxis(values, 0, 1).reshape(-1, blocks, EB)
            return jnp.moveaxis(values, 1, 0)

        parts, gathered = None, (by_block(wts), by_block(par), halo)
    marks, normed, inner, gate, gg, g, cs, act, proj, b_cols, c_cols, *own = front(
        L, cc, lengths, tokens, norm_gain, in_weight, out_weight, cotangent, parts, gathered
    )
    wts, par = gathered[:2] if gathered else own
    spre, dtk, u, entering, arriving = pre_scan(L, cc, proj, par, wts, act, g, marks, b_cols, c_cols)
    held, grad_c, block_out, grad_out, grad_in_gate, gn = fwd_scan(
        L, dtk, u, b_cols, c_cols, g, par, entering, act, gate, gg, out_weight, cotangent, tokens,
        normed, in_weight,
    )

    piece = 16 * sc
    fold = 2 if 2 * share <= piece else 1

    def owned(values):
        values = values.reshape(cc, -1, values.shape[-1] // fold)
        return jnp.pad(values, ((0, 0), (0, -values.shape[1] % piece), (0, 0)))

    def unfolded(values):
        if values.ndim == 2:
            return values[: share * fold].reshape(share, D)
        return values[:, : share * fold].reshape(2 * share, D)

    def by_owner(values):
        if share != EB:
            values = jnp.moveaxis(values, 0, 1).reshape(values.shape[1], cc, share)
            values = jnp.moveaxis(values, 1, 0)
        return jnp.pad(values, ((0, 0), (0, -values.shape[1] % piece), (0, 0)))

    early = [owned(grad_out), owned(grad_in_gate)]
    early_shapes = [v.shape for v in early]
    kinds = [None, cc // 2]
    sums = Sums(cc, sc, kinds, early_shapes, ["halve"] * 2, skew=3, pace=2)
    gap, chan_d, gproj, *early = bwd_scan(
        L, dtk, u, g, b_cols, c_cols, par, wts, arriving, held, spre, act, proj, grad_c, early, sums
    )
    gc, chan_e, after = conv_back(L, cc, gap, gproj, wts, act, cs, inner, marks)
    grad_in_inner, grad_tokens, grad_gain = tail(
        L, gc, after, par, marks, normed, in_weight, gn, tokens, cotangent, norm_gain
    )
    row = L.R + 2 * L.N + L.K + 1
    gain_part = jnp.pad(grad_gain.reshape(cc, 1, D // cc), ((0, 0), (0, 0), (0, share - D // cc)))
    chan_e = lax.dynamic_update_slice(by_owner(chan_e), gain_part.astype(bf16), (0, row, 0))
    late = [owned(grad_in_inner), by_owner(chan_d), chan_e]
    sum_inner, sum_d, sum_e, sum_out, sum_gate = sum_owned(
        late + early, [v.shape for v in late] + early_shapes, [0, None, None] + kinds,
        ["all"] * 3 + ["gather"] * 2, cc, sc,
    )
    sums = [unfolded(v) for v in (sum_inner, sum_gate, sum_out)] + [sum_d, sum_e]
    g_in, g_out, conv_w, conv_b, proj_w, step_w, step_b, decay, skip, g_gain = unpack(L, sums)
    return (
        block_out, grad_tokens, g_gain[: D // cc], g_in, conv_w, conv_b, proj_w.T, step_w,
        step_b, decay, skip, g_out,
    )


def solution(mesh):
    tok, row, vec = P(("seq", "chan"), None), P(None, "chan"), P("chan")
    in_specs = (
        tok, P(), P(), row, vec, P("chan", None), row, vec, row, vec, P(), tok, P("seq", None),
    )
    out_specs = (
        tok, tok, vec, row, row, vec, P("chan", None), row, vec, row, vec, P("chan", None),
    )
    return jax.shard_map(local, mesh=mesh, in_specs=in_specs, out_specs=out_specs, check_vma=False)
```

profile of v0, /device:TPU:0, one launch (start us, length us, event | category | flops | bytes accessed | tf_op | source)
XLA Modules:
  0.0 279.4 jit_solution(15155891258275541306)
XLA Ops:
  0.6 30.1 %front.1 = (f32[520,8]{1,0:T(8,128)}, bf16[512,768]{1,0:T(8,128)(2,1)}, bf16[528,1536]{1,0:T(8,128)(2,1)}, f32[512,1536]{1,0:T(8,128)}, f32[512,1536]{1,0:T(8,12...) custom-call(s32[1,4]{1,0:T(1,128)} %len_ref.1, ...), custom_call_target="tpu_custom_call" | custom-call | tf_op jit(solution)/shard_map/front/pallas_call | solution.py:274
  30.8 37.0 %pre_scan.1 = (f32[512,1536]{1,0:T(8,128)}, f32[512,1536]{1,0:T(8,128)}, f32[512,1536]{1,0:T(8,128)}, f32[16,1536]{1,0:T(8,128)}, f32[16,1536]{1,0:T(8,128)}) custom-call(f32[512,128]{1,0:T(8,128)} %get-tuple-element.62.proj_ref, f32[4,24,384]{2,1,0:T(8,128)} %get-tuple-element.63.par_ref, bf16[4,128,384]{2,1,0:T(8,128)(2,1)} %get-tuple-element.64.wts_ref, ...), custom_call_target="tpu_custom_call" | custom-call | tf_op jit(solution)/shard_map/pre_scan/pallas_call | solution.py:430
  67.8 45.6 %fwd_scan.1 = (bf16[8208,1536]{1,0:T(8,128)(2,1)}, f32[512,256]{1,0:T(8,128)}, bf16[512,768]{1,0:T(8,128)(2,1)}, bf16[1536,768]{1,0:T(8,128)(2,1)}, bf16[1536,768]{1,0:T(8,128)(2,1)}, /*index=5*/f32[512,768]{1,0:T(8,128)}) custom-call(f32[512,1536]{1,0:T(8,128)} %get-tuple-element.70.dtk_ref, f32[512,1536]{1,0:T(8,128)} %get-tuple-element.71.u_ref, ...), custom_call_target="tpu_custom_call" | custom-call | tf_op jit(solution)/shard_map/fwd_scan/pallas_call | solution.py:552
  113.4 62.3 %bwd_scan.1 = (f32[512,1536]{1,0:T(8,128)}, bf16[4,128,384]{2,1,0:T(8,128)(2,1)}, bf16[512,128]{1,0:T(8,128)(2,1)}, bf16[48,768]{1,0:T(8,128)(2,1)}, bf16[48,768]{1,0:T(8,128)(2,1)}) custom-call(f32[512,1536]{1,0:T(8,128)} %get-tuple-element.70.dtk_ref, f32[512,1536]{1,0:T(8,128)} %get-tuple-element.71.u_ref, f32[512,1536]{1,0:T(8,128)} %get-tuple-element.66.g_ref, ...), custom_call_target="tpu_custom_call" | custom-call | tf_op jit(solution)/shard_map/bwd_scan/pallas_call | solution.py:695
  175.7 14.6 %conv_back.1 = (f32[512,1536]{1,0:T(8,128)}, bf16[4,128,384]{2,1,0:T(8,128)(2,1)}, f32[8,1536]{1,0:T(8,128)}) custom-call(f32[512,1536]{1,0:T(8,128)} %get-tuple-element.83.gap_ref, bf16[512,128]{1,0:T(8,128)(2,1)} %get-tuple-element.84.gproj_ref, bf16[4,128,384]{2,1,0:T(8,128)(2,1)} %get-tuple-element.64.wts_ref, f32[512,1536]{1,0:T(8,128)} %get-tuple-element.65.act_ref, ...), custom_call_target="tpu_custom_call" | custom-call | tf_op jit(solution)/shard_map/conv_back/pallas_call | solution.py:783
  190.4 18.6 %tail.1 = (bf16[1536,768]{1,0:T(8,128)(2,1)}, f32[512,768]{1,0:T(8,128)}, f32[1,768]{1,0:T(1,128)}) custom-call(f32[512,1536]{1,0:T(8,128)} %get-tuple-element.87.gc_ref, f32[8,1536]{1,0:T(8,128)} %get-tuple-element.88.after_ref, f32[4,24,384]{2,1,0:T(8,128)} %get-tuple-element.63.par_ref, f32[520,8]{1,0:T(8,128)} %get-tuple-element.67.marks_ref, ...), custom_call_target="tpu_custom_call" | custom-call | tf_op jit(solution)/shard_map/tail/pallas_call | solution.py:861
  209.0 0.7 convert_reduce_fusion
  209.7 0.1 reshape.49
  209.8 1.4 dynamic_update_slice.3.refs_2_
  211.2 62.9 %sum_owned.1 = (bf16[2,384,768]{2,1,0:T(8,128)(2,1)}, bf16[128,384]{1,0:T(8,128)(2,1)}, bf16[128,384]{1,0:T(8,128)(2,1)}, bf16[384,768]{1,0:T(8,128)(2,1)}, bf16[2,384,768]{2,1,0:T(8,128)(2,1)}) custom-call(bf16[4,384,768]{2,1,0:T(8,128)(2,1)} %bitcast.9, bf16[4,128,384]{2,1,0:T(8,128)(2,1)} %get-tuple-element.92.refs_1_, ...), custom_call_target="tpu_custom_call" | custom-call | tf_op jit(solution)/shard_map/sum_owned/pallas_call | solution.py:1123
  274.1 4.1 %unpack.1 = (f32[768,768]{1,0:T(8,128)}, f32[384,768]{1,0:T(8,128)}, f32[4,384]{1,0:T(4,128)}, f32[384]{0:T(512)}, f32[80,384]{1,0:T(8,128)}, /*index=5*/f32[48,...) custom-call(bf16[768,768]{1,0:T(8,128)(2,1)} %bitcast.10, bf16[768,768]{1,0:T(8,128)(2,1)} %bitcast.11, ...), custom_call_target="tpu_custom_call" | custom-call | tf_op jit(solution)/shard_map/unpack/pallas_call | solution.py:1165
  278.2 1.2 slice.3
  (1 shorter events, 0.0 us)
where the time goes:
time: 280 us; the launch traced here: 279 us
  Pallas kernels  275 us (98%)
    pallas_call x1, Pallas kernels, sum_owned(): pl.pallas_call(functools.partial(sum_kernel, sums), in_specs=[vmem] * len...  62.9 us
    pallas_call x1, Pallas kernels, bwd_scan(): pl.pallas_call(functools.partial(bwd_kernel, L, sums, blocks), grid=(bloc...  62.3 us
    pallas_call x1, Pallas kernels, fwd_scan(): pl.pallas_call(functools.partial(fwd_kernel, L), grid=(blocks,), in_specs...  45.6 us
    pallas_call x1, Pallas kernels, pre_scan(): pl.pallas_call(functools.partial(pre_kernel, L, count), grid=(blocks,), i...  37 us
    pallas_call x1, Pallas kernels, front(): pl.pallas_call(functools.partial(front_kernel, L, count, inside), grid=(s...  30.1 us
    pallas_call x1, Pallas kernels, tail(): pl.pallas_call(functools.partial(tail_kernel, L), grid=(blocks,), in_spec...  18.6 us
    pallas_call x1, Pallas kernels, conv_back(): pl.pallas_call(functools.partial(conv_kernel, L, count), grid=(blocks,),...  14.6 us

commit v1 on v0

--- a/solution.py
+++ b/solution.py
@@ -11,7 +11,7 @@
 epsilon = 1e-05
 LOG2E = math.log2(math.e)
 CUT = 1e30
-TC = 16
+TC = 32
 EB = 384
 RT = 32
 BLOCK_SLOTS = 4
@@ -900,7 +900,7 @@
         )
 
     def span(self, p):
-        halvings = 1 + len(self.bits) + len(self.z_bits)
+        halvings = 2 + len(self.bits)
         phase = self.phases[self.pieces[p][0]]
         first = halvings if phase == "gather" else 0
         return first, halvings if phase == "halve" else len(self.stages(p))
@@ -917,13 +917,13 @@
 
     def final(self, p):
         a, first, width = self.pieces[p]
-        return pl.ds(first // (2 * self.size) * 16, 16)
+        return pl.ds(first // 4, self.size // 2)
 
     def outs(self):
         found = []
         for kind, dims, phase in zip(self.kinds, self.shapes, self.phases):
             if phase == "halve":
-                found.append(shape(bf16, dims[1] // (2 * self.size) * 16, dims[2]))
+                found.append(shape(bf16, dims[1] // 4, dims[2]))
             else:
                 found.append(shape(bf16, *(dims[1:] if kind is None else (2,) + tuple(dims[1:]))))
         return found
@@ -936,8 +936,7 @@
                 dims = (self.cc >> k, self.size, width)
                 found.append(pltpu.VMEM((1, 16, 128) if small else dims, bf16))
             for k in range(len(self.z_bits)):
-                dims = (self.size >> (k + 1), width)
-                found.append(pltpu.VMEM((16, 128) if small else dims, bf16))
+                found.append(pltpu.VMEM((self.size >> (k + 1), width), bf16))
             found.append(pltpu.VMEM((self.size, width), bf16))
         dims = (len(self.pieces), len(self.bits) + 2 * len(self.z_bits) + 3, max(2, self.cc // 2))
         return found + [pltpu.SemaphoreType.DMA(dims), pltpu.SemaphoreType.DMA(dims)]
@@ -1069,9 +1068,10 @@
         self.taking_part(p, s, work)
         if name in ("core", "chan", "z"):
             last = s == len(self.bits) + len(self.z_bits)
+            handed = self.phases[self.pieces[p][0]] == "halve" and self.span(p)[1] == s + 1
             for src, dst in zip(self.kept(p, s, True), self.landing(p, s)):
                 total = (dst[...].astype(f32) + src[...].astype(f32)).astype(bf16)
-                if last and self.span(p)[1] == s + 1:
+                if handed:
                     dst = self.o[self.pieces[p][0]].at[self.final(p), :]
                 elif last:
                     dst = self.gathered(p, len(self.z_bits))
@@ -1087,7 +1087,7 @@
             if first + 1 <= s <= end:
                 self.finish(p, s - 1)
             if first > 0 and s == first:
-                self.gathered(p, len(self.z_bits))[...] = self.x[self.pieces[p][0]][self.final(p), :]
+                self.held[p][first - 1][...] = self.x[self.pieces[p][0]][self.final(p), :]
             if first <= s < end:
                 self.start(p, s)
 
@@ -1227,7 +1227,7 @@
     early = [owned(grad_out), owned(grad_in_gate)]
     early_shapes = [v.shape for v in early]
     kinds = [None, cc // 2]
-    sums = Sums(cc, sc, kinds, early_shapes, ["halve"] * 2, skew=3, pace=2)
+    sums = Sums(cc, sc, kinds, early_shapes, ["halve"] * 2, skew=1, pace=3)
     gap, chan_d, gproj, *early = bwd_scan(
         L, dtk, u, g, b_cols, c_cols, par, wts, arriving, held, spre, act, proj, grad_c, early, sums
     )

time: 280 us -> 270 us (0.964)
  Pallas kernels: 275 us -> 266 us
    pallas_call x1, Pallas kernels: 45.6 us -> 42.4 us  [fwd_scan(): pl.pallas_call(functools.partial(fwd_kernel, L), grid=(blocks,), in_specs...]
    pallas_call x1, Pallas kernels: 62.3 us -> 59.2 us  [bwd_scan(): pl.pallas_call(functools.partial(bwd_kernel, L, sums, blocks), grid=(bloc...]
where the time goes in v1:
time: 270 us
  Pallas kernels  266 us (99%)
  local copies, waits for them, and re-layouts  2.72 us (1%)
    pallas_call x1, Pallas kernels, sum_owned(): pl.pallas_call(functools.partial(sum_kernel, sums), in_specs=[vmem] * len...  61.6 us
    pallas_call x1, Pallas kernels, bwd_scan(): pl.pallas_call(functools.partial(bwd_kernel, L, sums, blocks), grid=(bloc...  59.2 us
    pallas_call x1, Pallas kernels, fwd_scan(): pl.pallas_call(functools.partial(fwd_kernel, L), grid=(blocks,), in_specs...  42.4 us
    pallas_call x1, Pallas kernels, pre_scan(): pl.pallas_call(functools.partial(pre_kernel, L, count), grid=(blocks,), i...  34.3 us
    pallas_call x1, Pallas kernels, front(): pl.pallas_call(functools.partial(front_kernel, L, count, inside), grid=(s...  30 us
    pallas_call x1, Pallas kernels, tail(): pl.pallas_call(functools.partial(tail_kernel, L), grid=(blocks,), in_spec...  18.6 us
    pallas_call x1, Pallas kernels, conv_back(): pl.pallas_call(functools.partial(conv_kernel, L, count), grid=(blocks,),...  15.4 us

profile of v1, /device:TPU:0, one launch (start us, length us, event | category | flops | bytes accessed | tf_op | source)
XLA Modules:
  0.0 269.7 jit_solution(12130871426562721389)
XLA Ops:
  0.6 30.0 %front.1 = (f32[520,8]{1,0:T(8,128)}, bf16[512,768]{1,0:T(8,128)(2,1)}, bf16[528,1536]{1,0:T(8,128)(2,1)}, f32[512,1536]{1,0:T(8,128)}, f32[512,1536]{1,0:T(8,12...) custom-call(s32[1,4]{1,0:T(1,128)} %len_ref.1, ...), custom_call_target="tpu_custom_call" | custom-call | tf_op jit(solution)/shard_map/front/pallas_call | solution.py:274
  30.6 34.3 %pre_scan.1 = (f32[512,1536]{1,0:T(8,128)}, f32[512,1536]{1,0:T(8,128)}, f32[512,1536]{1,0:T(8,128)}, f32[16,1536]{1,0:T(8,128)}, f32[16,1536]{1,0:T(8,128)}) custom-call(f32[512,128]{1,0:T(8,128)} %get-tuple-element.62.proj_ref, f32[4,24,384]{2,1,0:T(8,128)} %get-tuple-element.63.par_ref, bf16[4,128,384]{2,1,0:T(8,128)(2,1)} %get-tuple-element.64.wts_ref, ...), custom_call_target="tpu_custom_call" | custom-call | tf_op jit(solution)/shard_map/pre_scan/pallas_call | solution.py:430
  64.9 42.4 %fwd_scan.1 = (bf16[8208,1536]{1,0:T(8,128)(2,1)}, f32[512,512]{1,0:T(8,128)}, bf16[512,768]{1,0:T(8,128)(2,1)}, bf16[1536,768]{1,0:T(8,128)(2,1)}, bf16[1536,768]{1,0:T(8,128)(2,1)}, /*index=5*/f32[512,768]{1,0:T(8,128)}) custom-call(f32[512,1536]{1,0:T(8,128)} %get-tuple-element.70.dtk_ref, f32[512,1536]{1,0:T(8,128)} %get-tuple-element.71.u_ref, ...), custom_call_target="tpu_custom_call" | custom-call | tf_op jit(solution)/shard_map/fwd_scan/pallas_call | solution.py:552
  107.3 59.2 %bwd_scan.1 = (f32[512,1536]{1,0:T(8,128)}, bf16[4,128,384]{2,1,0:T(8,128)(2,1)}, bf16[512,128]{1,0:T(8,128)(2,1)}, bf16[96,768]{1,0:T(8,128)(2,1)}, bf16[96,768]{1,0:T(8,128)(2,1)}) custom-call(f32[512,1536]{1,0:T(8,128)} %get-tuple-element.70.dtk_ref, f32[512,1536]{1,0:T(8,128)} %get-tuple-element.71.u_ref, f32[512,1536]{1,0:T(8,128)} %get-tuple-element.66.g_ref, ...), custom_call_target="tpu_custom_call" | custom-call | tf_op jit(solution)/shard_map/bwd_scan/pallas_call | solution.py:695
  166.6 15.4 %conv_back.1 = (f32[512,1536]{1,0:T(8,128)}, bf16[4,128,384]{2,1,0:T(8,128)(2,1)}, f32[8,1536]{1,0:T(8,128)}) custom-call(f32[512,1536]{1,0:T(8,128)} %get-tuple-element.83.gap_ref, bf16[512,128]{1,0:T(8,128)(2,1)} %get-tuple-element.84.gproj_ref, bf16[4,128,384]{2,1,0:T(8,128)(2,1)} %get-tuple-element.64.wts_ref, f32[512,1536]{1,0:T(8,128)} %get-tuple-element.65.act_ref, ...), custom_call_target="tpu_custom_call" | custom-call | tf_op jit(solution)/shard_map/conv_back/pallas_call | solution.py:783
  182.0 18.6 %tail.1 = (bf16[1536,768]{1,0:T(8,128)(2,1)}, f32[512,768]{1,0:T(8,128)}, f32[1,768]{1,0:T(1,128)}) custom-call(f32[512,1536]{1,0:T(8,128)} %get-tuple-element.87.gc_ref, f32[8,1536]{1,0:T(8,128)} %get-tuple-element.88.after_ref, f32[4,24,384]{2,1,0:T(8,128)} %get-tuple-element.63.par_ref, f32[520,8]{1,0:T(8,128)} %get-tuple-element.67.marks_ref, ...), custom_call_target="tpu_custom_call" | custom-call | tf_op jit(solution)/shard_map/tail/pallas_call | solution.py:861
  200.6 0.7 convert_reduce_fusion
  201.3 0.1 reshape.49
  201.4 1.4 dynamic_update_slice.3.refs_2_
  202.8 61.6 %sum_owned.1 = (bf16[2,384,768]{2,1,0:T(8,128)(2,1)}, bf16[128,384]{1,0:T(8,128)(2,1)}, bf16[128,384]{1,0:T(8,128)(2,1)}, bf16[384,768]{1,0:T(8,128)(2,1)}, bf16[2,384,768]{2,1,0:T(8,128)(2,1)}) custom-call(bf16[4,384,768]{2,1,0:T(8,128)(2,1)} %bitcast.9, bf16[4,128,384]{2,1,0:T(8,128)(2,1)} %get-tuple-element.92.refs_1_, ...), custom_call_target="tpu_custom_call" | custom-call | tf_op jit(solution)/shard_map/sum_owned/pallas_call | solution.py:1123
  264.4 4.1 %unpack.1 = (f32[768,768]{1,0:T(8,128)}, f32[384,768]{1,0:T(8,128)}, f32[4,384]{1,0:T(4,128)}, f32[384]{0:T(512)}, f32[80,384]{1,0:T(8,128)}, /*index=5*/f32[48,...) custom-call(bf16[768,768]{1,0:T(8,128)(2,1)} %bitcast.10, bf16[768,768]{1,0:T(8,128)(2,1)} %bitcast.11, ...), custom_call_target="tpu_custom_call" | custom-call | tf_op jit(solution)/shard_map/unpack/pallas_call | solution.py:1165
  268.5 1.2 slice.3
  (1 shorter events, 0.0 us)

commit v2 on v1

--- a/solution.py
+++ b/solution.py
@@ -11,7 +11,7 @@
 epsilon = 1e-05
 LOG2E = math.log2(math.e)
 CUT = 1e30
-TC = 32
+TC = 64
 EB = 384
 RT = 32
 BLOCK_SLOTS = 4
@@ -163,8 +163,9 @@
     given, refs = refs[: 7 if inside else 3], refs[7 if inside else 3 :]
     (
         marks_ref, normed_ref, inner_ref, gate_ref, gg_ref, g_ref, cs_ref, act_ref, proj_ref, bch_ref, cch_ref,
-    ) = refs[:11]
-    results, refs = refs[11 : 13 if inside else 11], refs[13 if inside else 11 :]
+        taps_ref,
+    ) = refs[:12]
+    results, refs = refs[12 : 14 if inside else 12], refs[14 if inside else 12 :]
     hn_ref, xs_ref, low_ref = refs[:3]
     T = tok_ref.shape[0]
     N, K = L.N, L.K
@@ -227,6 +228,7 @@
         c = slice(k * EB, (k + 1) * EB)
         taps = [par_ref[first + k, L.conv + j : L.conv + j + 1, :] for j in range(K)]
         bias = par_ref[first + k, L.conv_b : L.conv_b + 1, :]
+        taps_ref[:, c] = par_ref[first + k, L.conv : L.conv + 8, :]
 
         def tile(r, c=c, taps=taps, bias=bias):
             rows = pl.ds(r, RT)
@@ -279,11 +281,11 @@
             whole(T, D), whole(D), cols(D, wide), cols(D, wide, steps), tall(wide, D), whole(T, D),
         ] + given_specs,
         out_specs=[whole(T + 8, 8), whole(T, D), cols(T + HALO, wide)] + [cols(T, wide)] * 5 + [
-            whole(T, 128), whole(T // TC, N, TC), whole(T // TC, N, TC),
+            whole(T, 128), whole(T // TC, N, TC), whole(T // TC, N, TC), cols(8, wide),
         ] + [whole(*o.shape) for o in more_out],
         out_shape=[shape(f32, T + 8, 8), shape(bf16, T, D), shape(bf16, T + HALO, E)]
         + [shape(f32, T, E)] * 5
-        + [shape(f32, T, 128), shape(f32, T // TC, N, TC), shape(f32, T // TC, N, TC)]
+        + [shape(f32, T, 128), shape(f32, T // TC, N, TC), shape(f32, T // TC, N, TC), shape(f32, 8, E)]
         + more_out,
         scratch_shapes=[
             pltpu.VMEM((HALO, D), bf16),
@@ -876,10 +878,12 @@
 
 
 class Sums:
-    def __init__(self, chan_count, seq_count, kinds, shapes, phases, skew=1, pace=1):
+    def __init__(self, chan_count, seq_count, kinds, shapes, phases, skew=1, pace=1, begins=None, blocked=()):
         self.cc, self.sc = chan_count, seq_count
         self.kinds = kinds
         self.phases, self.skew, self.pace = phases, skew, pace
+        self.begins = begins
+        self.blocked = blocked
         self.size = 8 * seq_count
         self.bits = [1 << i for i in range(chan_count.bit_length() - 1)]
         self.z_bits = [2 << i for i in range(seq_count.bit_length() - 2)]
@@ -906,6 +910,8 @@
         return first, halvings if phase == "halve" else len(self.stages(p))
 
     def begin(self, p):
+        if self.begins is not None:
+            return self.begins[p]
         phase = self.phases[self.pieces[p][0]]
         before = [q for q in range(p) if self.phases[self.pieces[q][0]] == phase]
         return self.skew * (len(before) // 2)
@@ -924,6 +930,8 @@
         for kind, dims, phase in zip(self.kinds, self.shapes, self.phases):
             if phase == "halve":
                 found.append(shape(bf16, dims[1] // 4, dims[2]))
+            elif len(found) in self.blocked:
+                found.append(shape(bf16, 2 * dims[1], dims[2]))
             else:
                 found.append(shape(bf16, *(dims[1:] if kind is None else (2,) + tuple(dims[1:]))))
         return found
@@ -938,7 +946,7 @@
             for k in range(len(self.z_bits)):
                 found.append(pltpu.VMEM((self.size >> (k + 1), width), bf16))
             found.append(pltpu.VMEM((self.size, width), bf16))
-        dims = (len(self.pieces), len(self.bits) + 2 * len(self.z_bits) + 3, max(2, self.cc // 2))
+        dims = (len(self.pieces), len(self.bits) + 2 * len(self.z_bits) + 3, self.cc)
         return found + [pltpu.SemaphoreType.DMA(dims), pltpu.SemaphoreType.DMA(dims)]
 
     def bind(self, x_refs, o_refs, scratch):
@@ -1005,15 +1013,24 @@
         start = start + self.pieces[p][1] + self.core * self.size
         return self.o[self.pieces[p][0]].at[pl.ds(pl.multiple_of(start, 16), rows), :]
 
-    def places(self, p):
+    def target(self, p, v):
         a, first, width = self.pieces[p]
+        base = self.kinds[a]
+        if a in self.blocked:
+            row = first * self.cc + v * 2 * self.size
+            owner_rows = 2 * self.shapes[a][1]
+            rows = pl.ds(pl.multiple_of(row % owner_rows + self.core * self.size, 16), self.size)
+            return base + row // owner_rows, self.o[a].at[rows, :]
         rows = pl.ds(pl.multiple_of(first + self.core * self.size, 16), self.size)
-        return [self.o[a].at[b, rows, :] for b in range(2)] if self.half(p) else [self.o[a].at[rows, :]]
+        return base + v // 2, self.o[a].at[v % 2, rows, :]
 
     def move(self, p, s, v):
-        goal = self.kinds[self.pieces[p][0]] + v // 2
-        place = self.places(p)[v % 2]
-        return goal, place, self.copy(p, s, v % 2, self.held[p][-1], place, (self.si, goal))
+        goal, place = self.target(p, v)
+        return goal, place, self.copy(p, s, v, self.held[p][-1], place, (self.si, goal))
+
+    def pass_on(self, p, s, v):
+        goal, place = self.target(p, v)
+        return goal, self.copy(p, s, v, place, place, self.across(1))
 
     def copies(self, p, s):
         name, bit = self.stages(p)[s]
@@ -1022,17 +1039,16 @@
             device = device if name == "chan" else self.across(bit)
             pairs = zip(self.kept(p, s, False), self.landing(p, s))
             return [self.copy(p, s, i, src, dst, device) for i, (src, dst) in enumerate(pairs)]
-        places = self.places(p)
         if name == "zgather":
-            places = [self.gathered(p, self.z_bits.index(bit) + 1)]
-        return [self.copy(p, s, b, place, place, self.across(bit)) for b, place in enumerate(places)]
-
-    def taking_part(self, p, s, work):
-        if self.half(p) and self.stages(p)[s][0] == "cgather":
-            base = self.kinds[self.pieces[p][0]]
-            pl.when((self.ci >= base) & (self.ci < base + self.cc // 2))(work)
+            place = self.gathered(p, self.z_bits.index(bit) + 1)
         else:
-            work()
+            a, first, width = self.pieces[p]
+            rows = pl.ds(pl.multiple_of(first + self.core * self.size, 16), self.size)
+            place = self.o[a].at[rows, :]
+        return [self.copy(p, s, 0, place, place, self.across(bit))]
+
+    def last_of_half(self, p, s):
+        return self.half(p) and self.stages(p)[s][0] == "cgather"
 
     def start(self, p, s):
         if self.stages(p)[s][0] == "move":
@@ -1044,13 +1060,13 @@
                         place[...] = self.held[p][-1][...]
                     else:
                         copy.start()
-            return
-
-        def work():
+        elif self.last_of_half(p, s):
+            for v in range(self.cc):
+                goal, copy = self.pass_on(p, s, v)
+                pl.when(self.ci == goal)(copy.start)
+        else:
             for copy in self.copies(p, s):
                 copy.start()
-
-        self.taking_part(p, s, work)
 
     def finish(self, p, s):
         name, bit = self.stages(p)[s]
@@ -1060,12 +1076,13 @@
                 if goal != v:
                     pl.when(self.ci == goal)(copy.wait_recv)
             return
-
-        def work():
-            for copy in self.copies(p, s):
-                copy.wait_recv()
-
-        self.taking_part(p, s, work)
+        if self.last_of_half(p, s):
+            for v in range(self.cc):
+                goal, copy = self.pass_on(p, s, v)
+                pl.when(self.ci == goal)(copy.wait_recv)
+            return
+        for copy in self.copies(p, s):
+            copy.wait_recv()
         if name in ("core", "chan", "z"):
             last = s == len(self.bits) + len(self.z_bits)
             handed = self.phases[self.pieces[p][0]] == "halve" and self.span(p)[1] == s + 1
@@ -1099,13 +1116,23 @@
                         goal, place, copy = self.move(p, s, v)
                         if goal != v:
                             pl.when(self.ci == v)(copy.wait_send)
-                    continue
-
-                def work(p=p, s=s):
+                elif self.last_of_half(p, s):
+                    for v in range(self.cc):
+                        goal, copy = self.pass_on(p, s, v)
+                        pl.when(self.ci == goal)(copy.wait_send)
+                else:
                     for copy in self.copies(p, s):
                         copy.wait_send()
 
-                self.taking_part(p, s, work)
+    def hand_over(self, refs):
+        for kind, src, dst in zip(self.kinds, self.o, refs):
+            def work(src=src, dst=dst):
+                dst[...] = src[...]
+
+            if kind is None:
+                work()
+            else:
+                pl.when((self.ci >= kind) & (self.ci < kind + self.cc // 2))(work)
 
 
 def sum_kernel(sums, *refs):
@@ -1129,6 +1156,130 @@
         compiler_params=params(collective_id=0, has_side_effects=True),
         name="sum_owned",
     )(*arrays)
+
+
+def tail_sum_kernel(
+    L, sums, gain_row, gc_ref, after_ref, taps_ref, marks_ref, normed_ref, wi_ref, gn_ref, tok_ref, cot_ref, gain_ref,
+    d_ref, e_ref, *refs,
+):
+    early_refs, gtok_ref, refs = refs[:2], refs[2], refs[3:]
+    arrays = len(sums.kinds)
+    out_refs, held_refs, refs = refs[:arrays], refs[arrays : 2 * arrays], refs[2 * arrays :]
+    ext_ref, low_ref, sum_ref, xin_ref, xe_ref = refs[:5]
+    sums.bind((xin_ref, d_ref, xe_ref) + early_refs, held_refs, refs[5:])
+    T, D = tok_ref.shape
+    K, cc = L.K, sums.cc
+    i = pl.program_id(0)
+    blocks = xin_ref.shape[1] // (2 * sums.size)
+    width = low_ref.shape[1]
+
+    def tick_at(place):
+        for b in range(blocks):
+            pl.when(i == b)(functools.partial(sums.tick, 2 * b + place))
+
+    @pl.when(i == 0)
+    def _():
+        sums.barrier()
+        xe_ref[...] = e_ref[...]
+
+    tick_at(0)
+    ext_ref[0:T, :] = gc_ref[...]
+    ext_ref[T : T + 8, :] = after_ref[...]
+    taps = [taps_ref[j : j + 1, :] for j in range(K)]
+
+    def tile(r):
+        block = ext_ref[pl.ds(r, RT + 8), :]
+        marks = marks_ref[pl.ds(r, RT + 8), :]
+        total = taps[K - 1] * block[0:RT]
+        for j in range(1, K):
+            masked = block * marks[:, j - 1 : j]
+            total = total + taps[K - 1 - j] * masked[j : RT + j]
+        low_ref[pl.ds(r, RT), :] = total.astype(bf16)
+
+    row_tiles(T, tile)
+    tick_at(1)
+    grad = lax.dot_general(
+        low_ref[...], normed_ref[...], TN, preferred_element_type=f32
+    ).astype(bf16)
+    rows = pl.ds(pl.multiple_of(i * 2 * sums.size, 16), 2 * sums.size)
+    for v in range(cc):
+        xin_ref[v, rows, :] = grad[v * 2 * sums.size : (v + 1) * 2 * sums.size]
+    pl.when(i == blocks - 1)(functools.partial(sums.tick, 2 * blocks))
+    part = lax.dot_general(low_ref[...], wi_ref[...], NT, preferred_element_type=f32)
+
+    @pl.when(i == 0)
+    def _():
+        sum_ref[...] = gn_ref[...] + part
+
+    @pl.when(i > 0)
+    def _():
+        sum_ref[...] += part
+
+    @pl.when(i == blocks - 1)
+    def _():
+        gain = gain_ref[...].reshape(1, D)
+
+        def last(k, total):
+            rows = pl.ds(pl.multiple_of(k * 16, 16), 16)
+            x = tok_ref[rows, :].astype(f32)
+            grad = sum_ref[rows, :]
+            inv = lax.rsqrt(jnp.mean(x * x, axis=1, keepdims=True) + epsilon)
+            scaled = grad * gain
+            mean = jnp.mean(x * scaled, axis=1, keepdims=True)
+            gtok_ref[rows, :] = (
+                cot_ref[rows, :].astype(f32) + inv * scaled - x * (inv * inv * inv * mean)
+            )
+            return total + jnp.sum((grad * x * inv).reshape(2, 8, D), axis=0)
+
+        total = lax.fori_loop(0, T // 16, last, jnp.zeros((8, D), f32))
+        total = jnp.broadcast_to(jnp.sum(total, axis=0, keepdims=True), (16, D))
+        share, start = D // cc, gain_row // 16 * 16
+        dims = (16, xe_ref.shape[2])
+        here = lax.broadcasted_iota(jnp.int32, dims, 0) == gain_row - start
+        here = here & (lax.broadcasted_iota(jnp.int32, dims, 1) < share)
+        for q in range(cc):
+            turned = total if q == 0 else pltpu.roll(total, D - q * share, 1)
+            old = xe_ref[q, start : start + 16, :].astype(f32)
+            xe_ref[q, start : start + 16, :] = jnp.where(here, turned[:, : dims[1]], old).astype(bf16)
+        for n in range(2 * blocks + 1, sums.ticks()):
+            sums.tick(n)
+        sums.drain()
+        sums.hand_over(out_refs)
+
+
+def tail_sum(
+    L, counts, gc, after, taps, marks, normed, in_weight, gn, tokens, cot, gain, d, e, early, early_shapes, kinds,
+    gain_row,
+):
+    T, E = gc.shape
+    D = tokens.shape[1]
+    cc, sc = counts
+    piece = 16 * sc
+    wide = cc * piece
+    blocks = E // wide
+    shapes = [(cc, E // cc, D), d.shape, e.shape] + early_shapes
+    pieces = [v[1] // piece for v in shapes]
+    begins = [2 * (b + 1) for b in range(pieces[0])] + [0] * pieces[1] + [2 * blocks + 1] * pieces[2]
+    begins += [k // 2 for k in range(pieces[3] + pieces[4])]
+    sums = Sums(
+        cc, sc, [0, None, None] + kinds, shapes, ["all"] * 3 + ["gather"] * 2, begins=begins, blocked=(0,)
+    )
+    return pl.pallas_call(
+        functools.partial(tail_sum_kernel, L, sums, gain_row),
+        grid=(blocks,),
+        in_specs=[
+            cols(T, wide), cols(8, wide), cols(8, wide), whole(*marks.shape), whole(T, D), cols(D, wide),
+            whole(T, D), whole(T, D), whole(T, D), whole(D), once(*d.shape), once(*e.shape),
+        ] + [once(*v.shape) for v in early],
+        out_specs=[whole(T, D)] + [whole(*o.shape) for o in sums.outs()],
+        out_shape=[shape(f32, T, D)] + sums.outs(),
+        scratch_shapes=[pltpu.VMEM(o.shape, o.dtype) for o in sums.outs()] + [
+            pltpu.VMEM((T + 8, wide), f32), pltpu.VMEM((T, wide), bf16), pltpu.VMEM((T, D), f32),
+            pltpu.VMEM(shapes[0], bf16), pltpu.VMEM(e.shape, bf16),
+        ] + sums.scratch(),
+        compiler_params=params(collective_id=5, has_side_effects=True),
+        name="tail_sum",
+    )(gc, after, taps, marks, normed, in_weight, gn, tokens, cot, gain, d, e, *early)
 
 
 def unpack_kernel(L, inner_ref, gate_ref, out_ref, d_ref, e_ref, gin_ref, gout_ref, *refs):
@@ -1196,7 +1347,7 @@
             return jnp.moveaxis(values, 1, 0)
 
         parts, gathered = None, (by_block(wts), by_block(par), halo)
-    marks, normed, inner, gate, gg, g, cs, act, proj, b_cols, c_cols, *own = front(
+    marks, normed, inner, gate, gg, g, cs, act, proj, b_cols, c_cols, taps, *own = front(
         L, cc, lengths, tokens, norm_gain, in_weight, out_weight, cotangent, parts, gathered
     )
     wts, par = gathered[:2] if gathered else own
@@ -1232,18 +1383,26 @@
         L, dtk, u, g, b_cols, c_cols, par, wts, arriving, held, spre, act, proj, grad_c, early, sums
     )
     gc, chan_e, after = conv_back(L, cc, gap, gproj, wts, act, cs, inner, marks)
-    grad_in_inner, grad_tokens, grad_gain = tail(
-        L, gc, after, par, marks, normed, in_weight, gn, tokens, cotangent, norm_gain
-    )
     row = L.R + 2 * L.N + L.K + 1
-    gain_part = jnp.pad(grad_gain.reshape(cc, 1, D // cc), ((0, 0), (0, 0), (0, share - D // cc)))
-    chan_e = lax.dynamic_update_slice(by_owner(chan_e), gain_part.astype(bf16), (0, row, 0))
-    late = [owned(grad_in_inner), by_owner(chan_d), chan_e]
-    sum_inner, sum_d, sum_e, sum_out, sum_gate = sum_owned(
-        late + early, [v.shape for v in late] + early_shapes, [0, None, None] + kinds,
-        ["all"] * 3 + ["gather"] * 2, cc, sc,
-    )
-    sums = [unfolded(v) for v in (sum_inner, sum_gate, sum_out)] + [sum_d, sum_e]
+    chan_d, chan_e = by_owner(chan_d), by_owner(chan_e)
+    if share == EB and fold == 1 and E % (cc * piece) == 0:
+        grad_tokens, sum_inner, sum_d, sum_e, sum_out, sum_gate = tail_sum(
+            L, (cc, sc), gc, after, taps, marks, normed, in_weight, gn, tokens, cotangent, norm_gain,
+            chan_d, chan_e, early, early_shapes, kinds, row,
+        )
+    else:
+        grad_in_inner, grad_tokens, grad_gain = tail(
+            L, gc, after, par, marks, normed, in_weight, gn, tokens, cotangent, norm_gain
+        )
+        gain_part = jnp.pad(grad_gain.reshape(cc, 1, D // cc), ((0, 0), (0, 0), (0, share - D // cc)))
+        chan_e = lax.dynamic_update_slice(chan_e, gain_part.astype(bf16), (0, row, 0))
+        late = [owned(grad_in_inner), chan_d, chan_e]
+        sum_inner, sum_d, sum_e, sum_out, sum_gate = sum_owned(
+            late + early, [v.shape for v in late] + early_shapes, [0, None, None] + kinds,
+            ["all"] * 3 + ["gather"] * 2, cc, sc,
+        )
+        sum_inner = unfolded(sum_inner)
+    sums = [sum_inner, unfolded(sum_gate), unfolded(sum_out), sum_d, sum_e]
     g_in, g_out, conv_w, conv_b, proj_w, step_w, step_b, decay, skip, g_gain = unpack(L, sums)
     return (
         block_out, grad_tokens, g_gain[: D // cc], g_in, conv_w, conv_b, proj_w.T, step_w,

time: 270 us -> 270 us (level)
    pallas_call x1, Pallas kernels: 59.2 us -> 62.4 us  [bwd_scan(): pl.pallas_call(functools.partial(bwd_kernel, L, sums, blocks), grid=(bloc...]
    pallas_call x2 -> x1, Pallas kernels: 80.2 us -> 81 us  [tail_sum(): pl.pallas_call(functools.partial(tail_sum_kernel, L, sums, gain_row), gri...]
where the time goes in v2:
time: 270 us; the launch traced here: 269 us
  Pallas kernels  266 us (99%)
    pallas_call x1, Pallas kernels, tail_sum(): pl.pallas_call(functools.partial(tail_sum_kernel, L, sums, gain_row), gri...  81 us
    pallas_call x1, Pallas kernels, bwd_scan(): pl.pallas_call(functools.partial(bwd_kernel, L, sums, blocks), grid=(bloc...  62.4 us
    pallas_call x1, Pallas kernels, fwd_scan(): pl.pallas_call(functools.partial(fwd_kernel, L), grid=(blocks,), in_specs...  41 us
    pallas_call x1, Pallas kernels, pre_scan(): pl.pallas_call(functools.partial(pre_kernel, L, count), grid=(blocks,), i...  32.4 us
    pallas_call x1, Pallas kernels, front(): pl.pallas_call(functools.partial(front_kernel, L, count, inside), grid=(s...  29.9 us
    pallas_call x1, Pallas kernels, conv_back(): pl.pallas_call(functools.partial(conv_kernel, L, count), grid=(blocks,),...  15.4 us

profile of v2, /device:TPU:0, one launch (start us, length us, event | category | flops | bytes accessed | tf_op | source)
XLA Modules:
  0.0 269.3 jit_solution(16359066686166777808)
XLA Ops:
  0.6 29.9 %front.1 = (f32[520,8]{1,0:T(8,128)}, bf16[512,768]{1,0:T(8,128)(2,1)}, bf16[528,1536]{1,0:T(8,128)(2,1)}, f32[512,1536]{1,0:T(8,128)}, f32[512,1536]{1,0:T(8,12...) custom-call(s32[1,4]{1,0:T(1,128)} %len_ref.1, ...), custom_call_target="tpu_custom_call" | custom-call | tf_op jit(solution)/shard_map/front/pallas_call | solution.py:276
  30.5 32.4 %pre_scan.1 = (f32[512,1536]{1,0:T(8,128)}, f32[512,1536]{1,0:T(8,128)}, f32[512,1536]{1,0:T(8,128)}, f32[16,1536]{1,0:T(8,128)}, f32[16,1536]{1,0:T(8,128)}) custom-call(f32[512,128]{1,0:T(8,128)} %get-tuple-element.61.proj_ref, f32[4,24,384]{2,1,0:T(8,128)} %get-tuple-element.62.par_ref, bf16[4,128,384]{2,1,0:T(8,128)(2,1)} %get-tuple-element.63.wts_ref, ...), custom_call_target="tpu_custom_call" | custom-call | tf_op jit(solution)/shard_map/pre_scan/pallas_call | solution.py:432
  62.9 41.0 %fwd_scan.1 = (bf16[8208,1536]{1,0:T(8,128)(2,1)}, f32[512,1024]{1,0:T(8,128)}, bf16[512,768]{1,0:T(8,128)(2,1)}, bf16[1536,768]{1,0:T(8,128)(2,1)}, bf16[1536,768]{1,0:T(8,128)(2,1)}, /*index=5*/f32[512,768]{1,0:T(8,128)}) custom-call(f32[512,1536]{1,0:T(8,128)} %get-tuple-element.69.dtk_ref, f32[512,1536]{1,0:T(8,128)} %get-tuple-element.70.u_ref, ...), custom_call_target="tpu_custom_call" | custom-call | tf_op jit(solution)/shard_map/fwd_scan/pallas_call | solution.py:554
  103.9 62.4 %bwd_scan.1 = (f32[512,1536]{1,0:T(8,128)}, bf16[4,128,384]{2,1,0:T(8,128)(2,1)}, bf16[512,128]{1,0:T(8,128)(2,1)}, bf16[96,768]{1,0:T(8,128)(2,1)}, bf16[96,768]{1,0:T(8,128)(2,1)}) custom-call(f32[512,1536]{1,0:T(8,128)} %get-tuple-element.69.dtk_ref, f32[512,1536]{1,0:T(8,128)} %get-tuple-element.70.u_ref, f32[512,1536]{1,0:T(8,128)} %get-tuple-element.65.g_ref, ...), custom_call_target="tpu_custom_call" | custom-call | tf_op jit(solution)/shard_map/bwd_scan/pallas_call | solution.py:697
  166.3 15.4 %conv_back.1 = (f32[512,1536]{1,0:T(8,128)}, bf16[4,128,384]{2,1,0:T(8,128)(2,1)}, f32[8,1536]{1,0:T(8,128)}) custom-call(f32[512,1536]{1,0:T(8,128)} %get-tuple-element.82.gap_ref, bf16[512,128]{1,0:T(8,128)(2,1)} %get-tuple-element.83.gproj_ref, bf16[4,128,384]{2,1,0:T(8,128)(2,1)} %get-tuple-element.63.wts_ref, f32[512,1536]{1,0:T(8,128)} %get-tuple-element.64.act_ref, ...), custom_call_target="tpu_custom_call" | custom-call | tf_op jit(solution)/shard_map/conv_back/pallas_call | solution.py:785
  181.7 81.0 %tail_sum.1 = (f32[512,768]{1,0:T(8,128)}, bf16[768,768]{1,0:T(8,128)(2,1)}, bf16[128,384]{1,0:T(8,128)(2,1)}, bf16[128,384]{1,0:T(8,128)(2,1)}, bf16[384,768]{1,0:T(8,128)(2,1)}, /*index=5*/bf16[2,384,768]{2,1,0:T(8,128)(2,1)}) custom-call(f32[512,1536]{1,0:T(8,128)} %get-tuple-element.86.gc_ref, f32[8,1536]{1,0:T(8,128)} %get-tuple-element.87.after_ref, ...), custom_call_target="tpu_custom_call" | custom-call | tf_op jit(solution)/shard_map/tail_sum/pallas_call | solution.py:1267
  262.7 0.0 copy-start
  262.7 4.2 %unpack.1 = (f32[768,768]{1,0:T(8,128)}, f32[384,768]{1,0:T(8,128)}, f32[4,384]{1,0:T(4,128)}, f32[384]{0:T(512)}, f32[80,384]{1,0:T(8,128)}, /*index=5*/f32[48,...) custom-call(bf16[768,768]{1,0:T(8,128)(2,1)} %get-tuple-element.95.inner_ref, ...), custom_call_target="tpu_custom_call" | custom-call | tf_op jit(solution)/shard_map/unpack/pallas_call | solution.py:1316
  266.9 1.2 slice.3
  268.2 0.0 copy-done
  268.2 1.1 copy.26
Async XLA Ops:
  262.7 5.4 %copy-start = (f32[512,768]{1,0:T(8,128)S(1)}, f32[512,768]{1,0:T(8,128)}, u32[]{:S(2)}) copy-start(f32[512,768]{1,0:T(8,128)} %get-tuple-element.123) | copy-start | bytes 4718596

commit v3 on v2

--- a/solution.py
+++ b/solution.py
@@ -679,11 +679,9 @@
         diag = same_step(states, T)
         total = rank_ref[...]
         for ref, start in ((gb_ref, R), (gc_ref, R + states)):
-            fold = (target == state + start).astype(f32)
-            kept = jnp.where(diag, ref[...], 0.0)
-            total = total + jnp.dot(
-                kept, fold, precision=lax.Precision.HIGHEST, preferred_element_type=f32
-            )
+            fold = (target == state + start).astype(f32).astype(bf16)
+            kept = jnp.where(diag, ref[...], 0.0).astype(bf16)
+            total = total + jnp.dot(kept, fold, preferred_element_type=f32)
         gproj_ref[...] = total.astype(bf16)
         for n in range(blocks * BLOCK_SLOTS, sums.ticks()):
             sums.tick(n)

time: 270 us -> 266 us (0.985)
  Pallas kernels: 266 us -> 263 us
    pallas_call x1, Pallas kernels: 62.4 us -> 59 us  [bwd_scan(): pl.pallas_call(functools.partial(bwd_kernel, L, sums, blocks), grid=(bloc...]
where the time goes in v3:
time: 266 us
  Pallas kernels  263 us (99%)
    pallas_call x1, Pallas kernels, tail_sum(): pl.pallas_call(functools.partial(tail_sum_kernel, L, sums, gain_row), gri...  80.8 us
    pallas_call x1, Pallas kernels, bwd_scan(): pl.pallas_call(functools.partial(bwd_kernel, L, sums, blocks), grid=(bloc...  59 us
    pallas_call x1, Pallas kernels, fwd_scan(): pl.pallas_call(functools.partial(fwd_kernel, L), grid=(blocks,), in_specs...  41 us
    pallas_call x1, Pallas kernels, pre_scan(): pl.pallas_call(functools.partial(pre_kernel, L, count), grid=(blocks,), i...  32.4 us
    pallas_call x1, Pallas kernels, front(): pl.pallas_call(functools.partial(front_kernel, L, count, inside), grid=(s...  29.9 us
    pallas_call x1, Pallas kernels, conv_back(): pl.pallas_call(functools.partial(conv_kernel, L, count), grid=(blocks,),...  15.4 us

profile of v3, /device:TPU:0, one launch (start us, length us, event | category | flops | bytes accessed | tf_op | source)
XLA Modules:
  0.0 265.7 jit_solution(11053246194041316063)
XLA Ops:
  0.6 29.9 %front.1 = (f32[520,8]{1,0:T(8,128)}, bf16[512,768]{1,0:T(8,128)(2,1)}, bf16[528,1536]{1,0:T(8,128)(2,1)}, f32[512,1536]{1,0:T(8,128)}, f32[512,1536]{1,0:T(8,12...) custom-call(s32[1,4]{1,0:T(1,128)} %len_ref.1, ...), custom_call_target="tpu_custom_call" | custom-call | tf_op jit(solution)/shard_map/front/pallas_call | solution.py:276
  30.5 32.4 %pre_scan.1 = (f32[512,1536]{1,0:T(8,128)}, f32[512,1536]{1,0:T(8,128)}, f32[512,1536]{1,0:T(8,128)}, f32[16,1536]{1,0:T(8,128)}, f32[16,1536]{1,0:T(8,128)}) custom-call(f32[512,128]{1,0:T(8,128)} %get-tuple-element.61.proj_ref, f32[4,24,384]{2,1,0:T(8,128)} %get-tuple-element.62.par_ref, bf16[4,128,384]{2,1,0:T(8,128)(2,1)} %get-tuple-element.63.wts_ref, ...), custom_call_target="tpu_custom_call" | custom-call | tf_op jit(solution)/shard_map/pre_scan/pallas_call | solution.py:432
  62.9 41.0 %fwd_scan.1 = (bf16[8208,1536]{1,0:T(8,128)(2,1)}, f32[512,1024]{1,0:T(8,128)}, bf16[512,768]{1,0:T(8,128)(2,1)}, bf16[1536,768]{1,0:T(8,128)(2,1)}, bf16[1536,768]{1,0:T(8,128)(2,1)}, /*index=5*/f32[512,768]{1,0:T(8,128)}) custom-call(f32[512,1536]{1,0:T(8,128)} %get-tuple-element.69.dtk_ref, f32[512,1536]{1,0:T(8,128)} %get-tuple-element.70.u_ref, ...), custom_call_target="tpu_custom_call" | custom-call | tf_op jit(solution)/shard_map/fwd_scan/pallas_call | solution.py:554
  103.9 59.0 %bwd_scan.1 = (f32[512,1536]{1,0:T(8,128)}, bf16[4,128,384]{2,1,0:T(8,128)(2,1)}, bf16[512,128]{1,0:T(8,128)(2,1)}, bf16[96,768]{1,0:T(8,128)(2,1)}, bf16[96,768]{1,0:T(8,128)(2,1)}) custom-call(f32[512,1536]{1,0:T(8,128)} %get-tuple-element.69.dtk_ref, f32[512,1536]{1,0:T(8,128)} %get-tuple-element.70.u_ref, f32[512,1536]{1,0:T(8,128)} %get-tuple-element.65.g_ref, ...), custom_call_target="tpu_custom_call" | custom-call | tf_op jit(solution)/shard_map/bwd_scan/pallas_call | solution.py:695
  163.0 15.4 %conv_back.1 = (f32[512,1536]{1,0:T(8,128)}, bf16[4,128,384]{2,1,0:T(8,128)(2,1)}, f32[8,1536]{1,0:T(8,128)}) custom-call(f32[512,1536]{1,0:T(8,128)} %get-tuple-element.82.gap_ref, bf16[512,128]{1,0:T(8,128)(2,1)} %get-tuple-element.83.gproj_ref, bf16[4,128,384]{2,1,0:T(8,128)(2,1)} %get-tuple-element.63.wts_ref, f32[512,1536]{1,0:T(8,128)} %get-tuple-element.64.act_ref, ...), custom_call_target="tpu_custom_call" | custom-call | tf_op jit(solution)/shard_map/conv_back/pallas_call | solution.py:783
  178.3 80.8 %tail_sum.1 = (f32[512,768]{1,0:T(8,128)}, bf16[768,768]{1,0:T(8,128)(2,1)}, bf16[128,384]{1,0:T(8,128)(2,1)}, bf16[128,384]{1,0:T(8,128)(2,1)}, bf16[384,768]{1,0:T(8,128)(2,1)}, /*index=5*/bf16[2,384,768]{2,1,0:T(8,128)(2,1)}) custom-call(f32[512,1536]{1,0:T(8,128)} %get-tuple-element.86.gc_ref, f32[8,1536]{1,0:T(8,128)} %get-tuple-element.87.after_ref, ...), custom_call_target="tpu_custom_call" | custom-call | tf_op jit(solution)/shard_map/tail_sum/pallas_call | solution.py:1265
  259.2 0.0 copy-start
  259.2 4.2 %unpack.1 = (f32[768,768]{1,0:T(8,128)}, f32[384,768]{1,0:T(8,128)}, f32[4,384]{1,0:T(4,128)}, f32[384]{0:T(512)}, f32[80,384]{1,0:T(8,128)}, /*index=5*/f32[48,...) custom-call(bf16[768,768]{1,0:T(8,128)(2,1)} %get-tuple-element.95.inner_ref, ...), custom_call_target="tpu_custom_call" | custom-call | tf_op jit(solution)/shard_map/unpack/pallas_call | solution.py:1314
  263.3 1.2 slice.3
  264.6 0.0 copy-done
  264.6 1.1 copy.26
Async XLA Ops:
  259.2 5.4 %copy-start = (f32[512,768]{1,0:T(8,128)S(1)}, f32[512,768]{1,0:T(8,128)}, u32[]{:S(2)}) copy-start(f32[512,768]{1,0:T(8,128)} %get-tuple-element.123) | copy-start | bytes 4718596
